TPU v7x, 256 devices: a whole 4x4x8 slice. The times are simulated.
256 devices in a mesh: pair: 16 (over y, z_lo, core), virt: 16 (over z_hi, x).
Axes of the slice: x: 4, y: 4, z: 8 (z_hi: 4, z_lo: 2; z = z_hi * 2 + z_lo), core: 2. Of those that a mesh axis runs over, the one named last changes fastest.
Arguments:
- amplitudes: bfloat16 [24576, 4096], P('pair', 'virt'), may hold values from -6 to 6
- amp_map: int32 [192, 32], P('pair', 'virt'), may hold values 0 or 1
- integral_tiles: bfloat16 [128, 16, 128, 128], P('virt', 'pair'), may hold values from -0.25 to 0.25
- integral_cols: int32 [128, 16], P('virt'), may hold values from 0 to 31, all different within a row
- live_slots: int32 [128], P('virt'), may hold values from 1 to 16, 1280 in all
- pair_orbitals: int32 [2, 24576], P(None, 'pair'), may hold values from 0 to 1499
- virtual_pairs: int32 [2, 16384], P(None, 'virt'), may hold values from 0 to 11999
- occupied_energy: float32 [1500], replicated, may hold values from -1.5 to -0.3
- virtual_energy: float32 [12000], replicated, may hold values from 0.2 to 3
Outputs:
- ladder_update: bfloat16 [24576, 16384], P('pair', 'virt')
Inputs may be any that keep to these rules, and one draw needn't show every extreme that they name: `integral_cols`: row k lists 16 different amplitude column tiles; every column tile is listed by some row. Slot s of virtual-pair tile k is used when s < live_slots[k]; some tile uses all 16.
All inputs are finite; a program needn't handle non-finite values. No bound on the sum of `amp_map` or of `live_slots` on one device may be relied on, other than what follows from the above.
Results may differ from a plain program's by a relative error of at most 0.001.
Values may be sent and summed in bfloat16 or wider, within the bound.
No kernel may reach another device: no remote copies, remote signals or barrier semaphores. Data moves between devices by JAX's collectives and lax.ppermute only.
A program may use at most 128 MiB of HBM per device.

v0:
```python
import jax
import jax.numpy as jnp
from jax import lax
from jax.sharding import PartitionSpec as P


def pair_denominator(pair_orbitals, virtual_pairs, occupied_energy, virtual_energy):
    occupied_sum = jnp.take(occupied_energy, pair_orbitals[0]) + jnp.take(
        occupied_energy, pair_orbitals[1]
    )
    virtual_sum = jnp.take(virtual_energy, virtual_pairs[0]) + jnp.take(
        virtual_energy, virtual_pairs[1]
    )
    return virtual_sum[None, :] - occupied_sum[:, None]


def per_device(
    amplitudes,
    amp_map,
    integral_tiles,
    integral_cols,
    live_slots,
    pair_orbitals,
    virtual_pairs,
    occupied_energy,
    virtual_energy,
):
    pair_tiles, column_tiles = amp_map.shape
    tile_size = integral_tiles.shape[2]
    row_count = pair_tiles * tile_size
    ab_tiles = integral_tiles.shape[0]
    shaped = amplitudes.reshape(pair_tiles, tile_size, column_tiles, tile_size)
    masked = (shaped * amp_map.astype(jnp.bfloat16)[:, None, :, None]).reshape(
        row_count, column_tiles * tile_size
    )
    gathered_slots = lax.all_gather(integral_tiles, "pair", axis=1, tiled=True)
    slot_total = gathered_slots.shape[1]
    slot_live = lax.broadcasted_iota(jnp.int32, (ab_tiles, slot_total), 1) < live_slots[:, None]
    weights = jnp.where(slot_live[:, :, None, None], gathered_slots, jnp.zeros((), jnp.bfloat16))
    all_columns = column_tiles * lax.axis_size("virt")
    selector = (
        integral_cols[:, :, None] == lax.broadcasted_iota(jnp.int32, (1, 1, all_columns), 2)
    ).astype(jnp.bfloat16)
    dense_block = jnp.einsum(
        "ksc,ksxy->cxky", selector, weights, preferred_element_type=jnp.float32
    )
    dense_block = dense_block.astype(jnp.bfloat16).reshape(
        all_columns * tile_size, ab_tiles * tile_size
    )
    ladder = jnp.dot(
        lax.all_gather(masked, "virt", axis=1, tiled=True),
        dense_block,
        preferred_element_type=jnp.float32,
    )
    denominator = pair_denominator(pair_orbitals, virtual_pairs, occupied_energy, virtual_energy)
    return (ladder / denominator).astype(jnp.bfloat16)


def solution(mesh):
    placed = (
        P("pair", "virt"),
        P("pair", "virt"),
        P("virt", "pair", None, None),
        P("virt", None),
        P("virt"),
        P(None, "pair"),
        P(None, "virt"),
        P(),
        P(),
    )
    return jax.shard_map(
        per_device, mesh=mesh, in_specs=placed, out_specs=P("pair", "virt"), check_vma=False
    )
```

profile of v0, /device:TPU:32, one launch (start us, length us, event | category | flops | bytes accessed | tf_op | source)
XLA Modules:
  0.0 243.8 jit_solution(4561024064193788081)
XLA Ops:
  6.5 0.0 copy-start
  6.5 0.7 all-gather.5.cloned.1.call-update
  7.3 0.0 all-gather.3.cloned.1.call-start
  7.3 0.7 convert_element_type.13
  8.0 0.1 copy.12
  8.1 0.5 mul.11
  8.6 2.1 bitcast_multiply_fusion
  10.7 0.0 all-gather.3.cloned.1.call-update
  10.7 0.8 slice_reduce_fusion.1
  11.6 8.4 %gather_fusion.2 = f32[1536]{0:T(1024)S(1)} fusion(f32[1500]{0:T(1024)S(1)} %copy-done.1, s32[2048]{0:T(1024)S(1)} %pad_clamp_fusion.1), kind=kCustom, calls=%fused_computation.1.clone | custom fusion | bytes 18432 | tf_op jit(solution)/shard_map/jit(_take)/gather | solution.py:8
  20.0 0.0 copy-start.2
  20.0 8.4 %gather_fusion.3 = f32[1536]{0:T(1024)S(1)} fusion(f32[1500]{0:T(1024)S(1)} %copy-done.1, s32[2048]{0:T(1024)S(1)} %pad_clamp_fusion), kind=kCustom, calls=%fused_computation.3.clone | custom fusion | bytes 18432 | tf_op jit(solution)/shard_map/jit(_take)/gather | solution.py:8
  28.4 0.0 copy-start.4
  28.5 6.2 %gather_fusion = f32[1024]{0:T(1024)S(1)} fusion(f32[12000]{0:T(1024)S(1)} %copy-done, s32[1024]{0:T(1024)S(1)} %fusion.9), kind=kCustom, calls=%fused_computation.clone | custom fusion | bytes 12288 | tf_op jit(solution)/shard_map/jit(_take)/gather | solution.py:11
  34.7 0.0 copy-start.3
  34.7 6.2 %gather_fusion.1 = f32[1024]{0:T(1024)S(1)} fusion(f32[12000]{0:T(1024)S(1)} %copy-done, s32[1024]{0:T(1024)S(1)} %fusion.10), kind=kCustom, calls=%fused_computation.2.clone | custom fusion | bytes 12288 | tf_op jit(solution)/shard_map/jit(_take)/gather | solution.py:11
  40.8 0.1 iota_compare_fusion.1
  40.9 10.7 %all-gather.5.cloned.1.call-done = bf16[8,16,128,128]{3,2,1,0:T(8,128)(2,1)} async-done(((bf16[8,1,128,128]{3,2,1,0:T(8,128)(2,1)}), bf16[8,16,128,128]{3,2,1,0:T(8,128)(2,1)}) %all-gather.5.cloned.1.call-update) | async-done | bytes 4194320 | tf_op jit(solution)/shard_map/all_gather | solution.py:36
  51.6 2.5 %broadcast_select_fusion = bf16[8,16,128,128]{3,2,1,0:T(8,128)(2,1)S(1)} fusion(bf16[8,16,128,128]{3,2,1,0:T(8,128)(2,1)} %all-gather.5.cloned.1.call-done, pred[8,16]{1,0:T(8,128)(4,1)S(1)} %iota_compare_fusion.1), kind=kLoop, calls=%fused_computation.10 | loop fusion | flops 2097152 | bytes 8388736 | tf_op jit(solution)/shard_map/jit(_where)/select_n | solution.py:39
  54.2 0.0 copy-done.3
  54.2 6.7 %convert_bitcast_fusion = bf16[32,128,8,128]{3,0,1,2:T(8,128)(2,1)} fusion(bf16[8,16,128,128]{3,2,1,0:T(8,128)(2,1)S(1)} %broadcast_select_fusion, s32[8,16]{1,0:T(8,128)S(1)} %copy-done.3), kind=kOutput, calls=%fused_computation.7 | convolution fusion | flops 138416128 | bytes 12583424 | tf_op jit(solution)/shard_map/ksc,ksxy->cxky/dot_general | solution.py:44
  60.9 12.0 %copy.14 = bf16[32,128,8,128]{3,2,1,0:T(8,128)(2,1)} copy(bf16[32,128,8,128]{3,0,1,2:T(8,128)(2,1)} %convert_bitcast_fusion) | data formatting | bytes 16777216 | tf_op jit(solution)/shard_map/convert_element_type | solution.py:47
  72.9 145.0 %all-gather.3.cloned.1.call-done = bf16[1536,4096]{1,0:T(8,128)(2,1)} async-done(((bf16[1536,256]{1,0:T(8,128)(2,1)}), bf16[1536,4096]{1,0:T(8,128)(2,1)}) %all-gather.3.cloned.1.call-update) | async-done | bytes 12582928 | tf_op jit(solution)/shard_map/all_gather | solution.py:51
  217.8 19.1 %divide_convert_fusion = bf16[1536,1024]{1,0:T(8,128)(2,1)} fusion(bf16[1536,4096]{1,0:T(8,128)(2,1)} %all-gather.3.cloned.1.call-done, bf16[512,8,8,128]{3,2,1,0:T(8,128)(2,1)} %bitcast.21, f32[1536]{0:T(1024)S(1)} %select_add_fusion, f32[1024]{0:T(1024)S(1)} %select_add_fusion.1), kind=kOutput, calls=%fused_computation.8 | convolution fusion | flops 12889620480 | bytes 24127488 | tf_op jit(solution)/shard_map/dot_general | solution.py:50
  (14 shorter events, 0.1 us)
Async XLA Ops:
  6.5 21.9 %copy-start = (f32[12000]{0:T(1024)S(1)}, f32[12000]{0:T(1024)}, u32[]{:S(2)}) copy-start(f32[12000]{0:T(1024)} %param.21) | copy-start | bytes 144004
  6.5 5.1 %copy-start.1 = (f32[1500]{0:T(1024)S(1)}, f32[1500]{0:T(1024)}, u32[]{:S(2)}) copy-start(f32[1500]{0:T(1024)} %param.20) | copy-start | bytes 18004
  6.5 45.1 %all-gather.5.cloned.1.call-start = ((), (), s32[]{:S(2)}) async-start(), calls=%async_computation.1 | async-start | bytes 4456448 | tf_op jit(solution)/shard_map/all_gather | solution.py:36
  7.3 210.6 %all-gather.3.cloned.1.call-start = ((), (), s32[]{:S(2)}) async-start(), calls=%async_computation | async-start | bytes 13369344 | tf_op jit(solution)/shard_map/all_gather | solution.py:51
  20.0 8.4 %copy-start.2 = (s32[2,1024]{1,0:T(2,128)S(1)}, s32[2,1024]{1,0:T(2,128)}, u32[]{:S(2)}) copy-start(s32[2,1024]{1,0:T(2,128)} %param.19) | copy-start | bytes 24580
  28.4 12.4 %copy-start.4 = (s32[8]{0:T(128)S(1)}, s32[8]{0:T(128)}, u32[]{:S(2)}) copy-start(s32[8]{0:T(128)} %param.17) | copy-start | bytes 100
  34.7 19.5 %copy-start.3 = (s32[8,16]{1,0:T(8,128)S(1)}, s32[8,16]{1,0:T(8,128)}, u32[]{:S(2)}) copy-start(s32[8,16]{1,0:T(8,128)} %param.16) | copy-start | bytes 1540
Sparse Core Ops, SparseCore 0:
  9.2 42.3 all-gather.4
  54.0 163.7 all-gather.2
where the time goes:
time: 249 us; the launch traced here: 244 us
  waiting for transfers between devices  156 us (63%)
  local copies, waits for them, and re-layouts  42.5 us (17%)
  matrix products  25.9 us (10%)
  between operations  13.6 us (5%)
  other arithmetic  5.48 us (2%)
    all_gather x1, waiting for transfers between devices, per_device(): lax.all_gather(masked, 'virt', axis=1, tiled=True)  145 us
    dot_general x1, matrix products, per_device(): jnp.dot(lax.all_gather(masked, 'virt', axis=1, tiled=True), dense_block,...  19.1 us
    convert_element_type x1, local copies, waits for them, and re-layouts, per_device(): dense_block.astype(jnp.bfloat16)  12 us
    all_gather x1, waiting for transfers between devices, per_device(): gathered_slots = lax.all_gather(integral_tiles, 'pair', axis=1, tiled=True)  10.7 us
    gather x1, local copies, waits for them, and re-layouts, pair_denominator(): jnp.take(occupied_energy, pair_orbitals[1])  8.39 us
    gather x1, local copies, waits for them, and re-layouts, pair_denominator(): jnp.take(occupied_energy, pair_orbitals[0])  8.39 us
    dot_general x1, matrix products, per_device(): jnp.einsum('ksc,ksxy->cxky', selector, weights, preferred_element_type=jn...  6.71 us
    gather x1, local copies, waits for them, and re-layouts, pair_denominator(): jnp.take(virtual_energy, virtual_pairs[0])  6.15 us
  transfers between devices with their start and end apart: 2, of which 2 were waited for; matrix products, arithmetic and copies ran while one was open for 22% of the time, Pallas kernels for 0%

commit v1 on v0

v1 whole, which is shorter than its diff:
```python
import functools

import jax
import jax.numpy as jnp
import numpy as np
from jax import lax
from jax.experimental import pallas as pl
from jax.experimental.pallas import tpu as pltpu
from jax.sharding import PartitionSpec as P

ANY = pl.BlockSpec(memory_space=pl.ANY)
SMEM = pl.BlockSpec(memory_space=pltpu.SMEM)
VMEM = pl.BlockSpec(memory_space=pltpu.VMEM)
VMEM_LIMIT = 50 * 1024 * 1024
RING = 4
RING_ROWS = 832
GROUP = 4


def slot_table():
    table = np.zeros((16, 16), np.int32)
    for pair in range(16):
        y, zlo, core = pair // 4, pair // 2 % 2, pair % 2
        for local in range(16):
            which, dy, other = local // 8, local % 8 // 2, local % 2
            table[pair, local] = (y - dy) % 4 * 4 + (zlo ^ other) * 2 + (core ^ which)
    return table


def column_table(keys):
    return np.array(
        [
            [(virt // RING - dz) % RING * RING + (virt % RING - dx) % RING for dz, dx in keys]
            for virt in range(RING * RING)
        ],
        np.int32,
    )


def barrier(*arrays):
    return lax.optimization_barrier(arrays)


def after(array, *first):
    return lax.optimization_barrier((array,) + first)[0]


def virt_shift(array, dz, dx):
    pairs = [
        (z * RING + x, (z + dz) % RING * RING + (x + dx) % RING)
        for z in range(RING)
        for x in range(RING)
    ]
    return lax.ppermute(array, "virt", pairs)


def pair_shift(array, dy):
    return lax.ppermute(array, "pair", [(i, (i + 4 * dy) % 16) for i in range(16)])


def pair_swap(array, bit):
    return lax.ppermute(array, "pair", [(i, i ^ bit) for i in range(16)])


def table_lookup(table, index):
    rows = -(-table.shape[0] // 128)
    padded = jnp.zeros((rows * 128,), jnp.float32).at[: table.shape[0]].set(table).reshape(rows, 128)
    chosen = (index[:, None] // 128 == jnp.arange(rows, dtype=jnp.int32)[None, :]).astype(jnp.float32)
    lines = jnp.dot(chosen, padded, precision=lax.Precision.HIGHEST)
    lane = index[:, None] % 128 == jnp.arange(128, dtype=jnp.int32)[None, :]
    return jnp.sum(jnp.where(lane, lines, 0.0), axis=1)


def mask_kernel(amp_map, amplitudes, own, sent):
    split = own.shape[0]
    for tile in range(amp_map.shape[0]):
        for column in range(amp_map.shape[1]):
            keep = amp_map[tile, column].astype(jnp.float32).astype(jnp.bfloat16)
            lanes = slice(column * 128, column * 128 + 128)
            first, last = tile * 128, tile * 128 + 128
            middle = min(max(split, first), last)
            if first < middle:
                own[first:middle, lanes] = amplitudes[first:middle, lanes] * keep
            if middle < last:
                sent[middle - split : last - split, lanes] = amplitudes[middle:last, lanes] * keep


def mask(amplitudes, amp_map, rows):
    count, columns = amplitudes.shape
    return pl.pallas_call(
        mask_kernel,
        in_specs=[SMEM, VMEM],
        out_specs=[VMEM, VMEM],
        out_shape=[
            jax.ShapeDtypeStruct((rows, columns), jnp.bfloat16),
            jax.ShapeDtypeStruct((count - rows, columns), jnp.bfloat16),
        ],
    )(amp_map, amplitudes)


def weights_kernel(slots, cols, live, mine, theirs, out):
    tile = pl.program_id(0)
    out[...] = jnp.zeros_like(out)
    for local in range(16):
        slot = slots[local]
        source = mine if local < 8 else theirs

        @pl.when(slot < live[tile])
        def _(local=local, slot=slot, source=source):
            row = pl.multiple_of(cols[tile, slot] * 128, 128)
            out[pl.ds(row, 128), :] = source[0, local % 8]


def dense_weights(slots, cols, live, mine, theirs):
    tiles = cols.shape[0]
    block = pl.BlockSpec((1, 8, 128, 128), lambda k: (k, 0, 0, 0))
    return pl.pallas_call(
        weights_kernel,
        grid=(tiles,),
        in_specs=[SMEM] * 3 + [block] * 2,
        out_specs=pl.BlockSpec((4096, 128), lambda k: (0, k)),
        out_shape=jax.ShapeDtypeStruct((4096, tiles * 128), jnp.bfloat16),
        cost_estimate=pl.CostEstimate(flops=0, bytes_accessed=tiles * 24 * 2**16, transcendentals=0),
        compiler_params=pltpu.CompilerParams(vmem_limit_bytes=VMEM_LIMIT),
    )(slots, cols, live, mine, theirs)


def matmul_kernel(plan, piece_count, rows, row0, has_total, final, has_base, *refs):
    refs = list(refs)
    where, weights = refs[:2]
    pieces = refs[2 : 2 + piece_count]
    rest = refs[2 + len(pieces) :]
    total_in = rest.pop(0) if has_total else None
    if final:
        virtual_sum, pair_energy = rest.pop(0), rest.pop(0)
    if has_base:
        rest.pop(0)
    out = rest.pop(0)
    held, wheld, total = rest[:3]
    held_sem, w_sem, total_sem, out_sem = rest[3:7]
    staged = rest[7] if final else None
    count = len(plan)
    if has_total:
        load_total = pltpu.make_async_copy(total_in, total, total_sem)
        load_total.start()
    for j, parts in enumerate(plan):
        for piece, first, start, size in parts:
            source = pieces[piece]
            source = source.at[first] if len(source.shape) == 3 else source.at[pl.ds(first, size)]
            pltpu.make_async_copy(
                source, held.at[pl.ds(start, size), pl.ds(j * 256, 256)], held_sem.at[j]
            ).start()
        pltpu.make_async_copy(
            weights.at[pl.ds(pl.multiple_of(where[j] * 256, 256), 256)],
            wheld.at[pl.ds(j * 256, 256)],
            w_sem.at[j],
        ).start()
    if has_total:
        load_total.wait()
    for group in range(0, count, GROUP):
        last = min(group + GROUP, count)
        for j in range(group, last):
            slot = held.at[:, pl.ds(j * 256, 256)]
            pltpu.make_async_copy(slot, slot, held_sem.at[j]).wait()
            wslot = wheld.at[pl.ds(j * 256, 256)]
            pltpu.make_async_copy(wslot, wslot, w_sem.at[j]).wait()
        first = group == 0 and not has_total
        ends = last == count

        product = jnp.dot(
            held[:, group * 256 : last * 256],
            wheld[group * 256 : last * 256, :],
            preferred_element_type=jnp.float32,
        )
        if not first:
            product = total[...] + product
        if ends and final:
            staged[...] = (product / (virtual_sum[...] - pair_energy[...])).astype(jnp.bfloat16)
        else:
            total[...] = product
    if final:
        store = pltpu.make_async_copy(staged, out.at[pl.ds(row0, rows)], out_sem)
    else:
        store = pltpu.make_async_copy(total, out, out_sem)
    store.start()
    store.wait()


def block_matmul(where, weights, plan, pieces, rows, row0=0, all_rows=0, total=None, energies=None, base=None):
    columns = weights.shape[1]
    count = len(plan)
    final = energies is not None
    operands = [where, weights] + list(pieces)
    specs = [SMEM] + [ANY] * (1 + len(pieces))
    if total is not None:
        operands.append(total)
        specs.append(ANY)
    if final:
        operands += list(energies)
        specs += [VMEM, VMEM]
    aliases = {}
    if base is not None:
        aliases = {len(operands): 0}
        operands.append(base)
        specs.append(ANY)
    shape = (all_rows, columns) if final else (rows, columns)
    kind = jnp.bfloat16 if final else jnp.float32
    scratch = [
        pltpu.VMEM((rows, count * 256), jnp.bfloat16),
        pltpu.VMEM((count * 256, columns), jnp.bfloat16),
        pltpu.VMEM((rows, columns), jnp.float32),
        pltpu.SemaphoreType.DMA((count,)),
        pltpu.SemaphoreType.DMA((count,)),
        pltpu.SemaphoreType.DMA,
        pltpu.SemaphoreType.DMA,
    ]
    if final:
        scratch.append(pltpu.VMEM((rows, columns), jnp.bfloat16))
    return pl.pallas_call(
        functools.partial(matmul_kernel, plan, len(pieces), rows, row0, total is not None, final, base is not None),
        in_specs=specs,
        out_specs=ANY,
        out_shape=jax.ShapeDtypeStruct(shape, kind),
        scratch_shapes=scratch,
        input_output_aliases=aliases,
        cost_estimate=pl.CostEstimate(
            flops=2 * rows * count * 256 * columns,
            bytes_accessed=(rows + columns) * count * 512 + rows * columns * 8,
            transcendentals=0,
        ),
        compiler_params=pltpu.CompilerParams(vmem_limit_bytes=VMEM_LIMIT),
    )(*operands)


def per_device(
    amplitudes,
    amp_map,
    integral_tiles,
    integral_cols,
    live_slots,
    pair_orbitals,
    virtual_pairs,
    occupied_energy,
    virtual_energy,
):
    row_count = amplitudes.shape[0]
    rows = RING_ROWS
    gather_rows = row_count - rows
    half = rows // 2
    own, sent = mask(amplitudes, amp_map, rows)

    pair = lax.axis_index("pair")
    virt = lax.axis_index("virt")

    gathered = lax.all_gather(sent, "virt", axis=0)

    two = jnp.concatenate([integral_tiles, pair_swap(integral_tiles, 2)], axis=1)
    own, two = barrier(own, two)
    x1, x3 = virt_shift(own, 0, 1), virt_shift(own, 0, -1)
    z1, z3, x1, x3, x2a, x2b, y1, y2, y3 = barrier(
        virt_shift(own, 1, 0),
        virt_shift(own, -1, 0),
        x1,
        x3,
        virt_shift(x1[:half], 0, 1),
        virt_shift(x3[half:], 0, -1),
        pair_shift(two, 1),
        pair_shift(two, 2),
        pair_shift(two, -1),
    )
    mine = jnp.concatenate([two, y1, y2, y3], axis=1)
    near = jnp.concatenate([z1, z3])
    z2a, z2b, right, left, theirs = barrier(
        virt_shift(z1[:half], 1, 0),
        virt_shift(z3[half:], -1, 0),
        virt_shift(near, 0, 1),
        virt_shift(near, 0, -1),
        pair_swap(mine, 1),
    )
    weights = dense_weights(jnp.asarray(slot_table())[pair], integral_cols, live_slots, mine, theirs)

    right2, left2 = barrier(
        virt_shift(jnp.concatenate([right[:rows], z2a, z2b]), 0, 1),
        virt_shift(jnp.concatenate([left[rows:], z2a, z2b]), 0, -1),
    )
    def whole(array, first=0):
        return [(array, first, 0, rows)]

    def halves(low, low_first, high, high_first):
        return [(low, low_first, 0, half), (high, high_first, half, half)]

    block = {
        (0, 0): whole(own),
        (1, 0): whole(z1),
        (3, 0): whole(z3),
        (0, 1): whole(x1),
        (0, 3): whole(x3),
        (2, 0): halves(z2a, 0, z2b, 0),
        (0, 2): halves(x2a, 0, x2b, 0),
        (1, 1): whole(right),
        (3, 1): whole(right, rows),
        (1, 3): whole(left),
        (3, 3): whole(left, rows),
    }

    pair_orbitals, virtual_pairs = after(pair_orbitals, z1), after(virtual_pairs, z1)
    occupied = table_lookup(occupied_energy, pair_orbitals.reshape(-1)).reshape(2, -1)
    virtual = table_lookup(virtual_energy, virtual_pairs.reshape(-1)).reshape(2, -1)
    pair_energy = (occupied[0] + occupied[1])[:, None]
    virtual_sum = (virtual[0] + virtual[1])[None, :]

    def multiply(keys, **options):
        where = jnp.asarray(column_table(keys))[virt]
        plan, pieces, seen = [], [], {}
        for key in keys:
            parts = []
            for array, first, start, size in block[key]:
                if id(array) not in seen:
                    seen[id(array)] = len(pieces)
                    pieces.append(array)
                parts.append((seen[id(array)], first, start, size))
            plan.append(tuple(parts))
        return block_matmul(where, weights, tuple(plan), pieces, rows, **options)

    early = [(0, 0), (1, 0), (3, 0), (0, 1), (0, 3), (2, 0), (0, 2), (1, 1), (1, 3), (3, 1), (3, 3)]
    late = [(1, 2), (3, 2), (2, 1), (2, 3)]
    total = multiply(early)
    right2, left2, total = barrier(right2, left2, total)
    right3 = virt_shift(right2[rows : rows + half], 0, 1)
    left3 = virt_shift(left2[rows + half :], 0, -1)
    block.update(
        {
            (1, 2): whole(right2),
            (3, 2): whole(left2),
            (2, 1): halves(right2, rows, right2, rows + half),
            (2, 3): halves(left2, rows, left2, rows + half),
            (2, 2): halves(right3, 0, left3, 0),
        }
    )
    total = multiply(late, total=total)
    result = block_matmul(
        jnp.arange(16, dtype=jnp.int32),
        weights,
        tuple(((0, v, 0, gather_rows),) for v in range(16)),
        [gathered],
        gather_rows,
        row0=rows,
        all_rows=row_count,
        energies=(virtual_sum, pair_energy[rows:]),
    )
    return multiply(
        [(2, 2)],
        total=total,
        energies=(virtual_sum, pair_energy[:rows]),
        all_rows=row_count,
        base=result,
    )


def solution(mesh):
    placed = (
        P("pair", "virt"),
        P("pair", "virt"),
        P("virt", "pair", None, None),
        P("virt", None),
        P("virt"),
        P(None, "pair"),
        P(None, "virt"),
        P(),
        P(),
    )
    return jax.shard_map(
        per_device, mesh=mesh, in_specs=placed, out_specs=P("pair", "virt"), check_vma=False
    )
```

time: 249 us -> 170 us (0.68); the launches traced: 244 us -> 170 us
  waiting for transfers between devices: 156 us -> 65.1 us
  Pallas kernels: 0 us -> 41.9 us
  starting transfers between devices: 0.04 us -> 34.2 us
  local copies, waits for them, and re-layouts: 42.5 us -> 11.4 us
  matrix products: 25.9 us -> 2.15 us
  other arithmetic: 5.48 us -> 1.15 us
    all_gather x2 -> x1, waiting for transfers between devices: 156 us -> 0.02 us  [per_device(): gathered = lax.all_gather(sent, 'virt', axis=0)]
    ppermute x0 -> x19, waiting for transfers between devices: none -> 65.1 us  [the longest x14 58.7 us: virt_shift(): return lax.ppermute(array, 'virt', pairs)]
    pallas_call x0 -> x6, Pallas kernels: none -> 41.9 us  [the longest x4 31.5 us: block_matmul(): pl.pallas_call(functools.partial(matmul_kernel, plan, len(pieces), rows,...]
    ppermute x0 -> x19, starting transfers between devices: none -> 34.2 us  [the longest x14 26.3 us: virt_shift(): return lax.ppermute(array, 'virt', pairs)]
    gather x4 -> x0, local copies, waits for them, and re-layouts: 29.1 us -> none  [the longest x1 8.39 us: pair_denominator(): jnp.take(occupied_energy, pair_orbitals[1])]
    dot_general x2, matrix products: 25.9 us -> 2.15 us  [table_lookup(): lines = jnp.dot(chosen, padded, precision=lax.Precision.HIGHEST)]
    convert_element_type x2 -> x0, local copies, waits for them, and re-layouts: 12.1 us -> none  [the longest x1 12 us: per_device(): dense_block.astype(jnp.bfloat16)]
    slice x2 -> x12, local copies, waits for them, and re-layouts: 0.83 us -> 4.85 us  [the longest x1 1.18 us: per_device(): left[rows:]]
  transfers between devices with their start and end apart: 2 -> 20, of which waited for: 2 -> 6; matrix products, arithmetic and copies ran while one was open for 22% -> 8% of each run, Pallas kernels for 0% -> 21%
where the time goes in v1:
time: 170 us
  waiting for transfers between devices  65.1 us (38%)
  Pallas kernels  41.9 us (25%)
  starting transfers between devices  34.2 us (20%)
  between operations  13.9 us (8%)
  local copies, waits for them, and re-layouts  11.4 us (7%)
  matrix products  2.15 us (1%)
    ppermute x14, waiting for transfers between devices, virt_shift(): return lax.ppermute(array, 'virt', pairs)  58.7 us
    pallas_call x4, Pallas kernels, block_matmul(): pl.pallas_call(functools.partial(matmul_kernel, plan, len(pieces), rows,...  31.5 us
    ppermute x14, starting transfers between devices, virt_shift(): return lax.ppermute(array, 'virt', pairs)  26.3 us
    pallas_call x1, Pallas kernels, dense_weights(): pl.pallas_call(weights_kernel, grid=(tiles,), in_specs=[SMEM] * 3 + [bloc...  8.19 us
    ppermute x2, waiting for transfers between devices, pair_swap(): return lax.ppermute(array, 'pair', [(i, i ^ bit) for i in range(16)])  6.41 us
    ppermute x3, starting transfers between devices, pair_shift(): lax.ppermute(array, 'pair', [(i, (i + 4 * dy) % 16) for i in range(16)])  5.83 us
  transfers between devices with their start and end apart: 20, of which 6 were waited for; matrix products, arithmetic and copies ran while one was open for 8% of the time, Pallas kernels for 21%

profile of v1, /device:TPU:32, one launch (start us, length us, event | category | flops | bytes accessed | tf_op | source)
XLA Modules:
  0.0 169.8 jit_solution(7137012935900079635)
XLA Ops:
  7.9 2.2 %shard_map.127 = (bf16[832,256]{1,0:T(8,128)(2,1)}, bf16[704,256]{1,0:T(8,128)(2,1)}) custom-call(s32[12,2]{1,0:T(8,128)} %copy.19.amp_map, bf16[1536,256]{1,0:T(8,128)(2,1)} %amplitudes.1), custom_call_target="tpu_custom_call" | custom-call | tf_op jit(solution)/shard_map/pallas_call | solution.py:90
  10.1 1.9 %collective-permute-start = (bf16[8,1,128,128]{3,2,1,0:T(8,128)(2,1)}, bf16[8,1,128,128]{3,2,1,0:T(8,128)(2,1)S(1)}, u32[]{:S(2)}, u32[]{:S(2)}) collective-permute-start(bf16[8,1,128,128]{3,2,1,0:T(8,128)(2,1)} %param.19), channel_id=1, source_target_pairs={{0,32},{16,48},{32,0},{48,16},{64,96},{80,112},{96,64},{112,80},{1... | collective-permute-start | bytes 786440 | tf_op jit(solution)/shard_map/ppermute | solution.py:62
  12.0 6.4 %collective-permute-done = bf16[8,1,128,128]{3,2,1,0:T(8,128)(2,1)S(1)} collective-permute-done((bf16[8,1,128,128]{3,2,1,0:T(8,128)(2,1)}, bf16[8,1,128,128]{3,2,1,0:T(8,128)(2,1)S(1)}, u32[]{:S(2)}, u32[]{:S(2)}) %collective-permute-start) | collective-permute-done | bytes 262176 | tf_op jit(solution)/shard_map/ppermute | solution.py:62
  19.5 1.6 collective-permute-start.3
  21.0 1.7 %collective-permute-start.4 = (bf16[832,256]{1,0:T(8,128)(2,1)}, bf16[832,256]{1,0:T(8,128)(2,1)S(1)}, u32[]{:S(2)}, u32[]{:S(2)}) collective-permute-start(bf16[832,256]{1,0:T(8,128)(2,1)} %get-tuple-element.56.refs_2_), channel_id=1, source_target_pairs={{0,3},{1,0},{2,1},{3,2},{4,7},{5,4},{6,5},{7,6},{8,11},{9,8},{10,9... | collective-permute-start | bytes 1277960 | tf_op jit(solution)/shard_map/ppermute | solution.py:54
  22.8 3.3 %collective-permute-start.1 = (bf16[832,256]{1,0:T(8,128)(2,1)}, bf16[832,256]{1,0:T(8,128)(2,1)S(1)}, u32[]{:S(2)}, u32[]{:S(2)}) collective-permute-start(bf16[832,256]{1,0:T(8,128)(2,1)} %get-tuple-element.56.refs_2_), channel_id=1, source_target_pairs={{0,4},{1,5},{2,6},{3,7},{4,8},{5,9},{6,10},{7,11},{8,12},{9,13},{1... | collective-permute-start | bytes 1277960 | tf_op jit(solution)/shard_map/ppermute | solution.py:54
  26.0 2.1 %collective-permute-start.2 = (bf16[832,256]{1,0:T(8,128)(2,1)}, bf16[832,256]{1,0:T(8,128)(2,1)S(1)}, u32[]{:S(2)}, u32[]{:S(2)}) collective-permute-start(bf16[832,256]{1,0:T(8,128)(2,1)} %get-tuple-element.56.refs_2_), channel_id=1, source_target_pairs={{0,12},{1,13},{2,14},{3,15},{4,0},{5,1},{6,2},{7,3},{8,4},{9,5},{1... | collective-permute-start | bytes 1277960 | tf_op jit(solution)/shard_map/ppermute | solution.py:54
  28.2 1.6 collective-permute-start.7
  29.8 4.3 %collective-permute-done.3.refs_5_ = bf16[832,256]{1,0:T(8,128)(2,1)S(1)} collective-permute-done((bf16[832,256]{1,0:T(8,128)(2,1)}, bf16[832,256]{1,0:T(8,128)(2,1)S(1)}, u32[]{:S(2)}, u32[]{:S(2)}) %collective-permute-start.3) | collective-permute-done | bytes 426016 | tf_op jit(solution)/shard_map/ppermute | solution.py:54
  34.1 3.2 %collective-permute-start.8 = (bf16[8,2,128,128]{3,2,1,0:T(8,128)(2,1)S(1)}, bf16[8,2,128,128]{3,2,1,0:T(8,128)(2,1)S(1)}, u32[]{:S(2)}, u32[]{:S(2)}) collective-permute-start(bf16[8,2,128,128]{3,2,1,0:T(8,128)(2,1)S(1)} %pad_maximum_fusion.4), channel_id=1, source_target_pairs={{0,128},{16,144},{32,160},{48,176},{64,192},{80,208},{96,224},{112... | collective-permute-start | bytes 1572872 | tf_op jit(solution)/shard_map/ppermute | solution.py:58
  38.4 18.9 %collective-permute-done.1.refs_3_ = bf16[832,256]{1,0:T(8,128)(2,1)S(1)} collective-permute-done((bf16[832,256]{1,0:T(8,128)(2,1)}, bf16[832,256]{1,0:T(8,128)(2,1)S(1)}, u32[]{:S(2)}, u32[]{:S(2)}) %collective-permute-start.1) | collective-permute-done | bytes 426016 | tf_op jit(solution)/shard_map/ppermute | solution.py:54
  57.3 3.3 %collective-permute-start.6 = (bf16[416,256]{1,0:T(8,128)(2,1)S(1)}, bf16[416,256]{1,0:T(8,128)(2,1)S(1)}, u32[]{:S(2)}, u32[]{:S(2)}) collective-permute-start(bf16[416,256]{1,0:T(8,128)(2,1)S(1)} %slice.93), channel_id=1, source_target_pairs={{0,3},{1,0},{2,1},{3,2},{4,7},{5,4},{6,5},{7,6},{8,11},{9,8},{10,9... | collective-permute-start | bytes 638984 | tf_op jit(solution)/shard_map/ppermute | solution.py:54
  60.7 4.4 %collective-permute-done.5.refs_9_ = bf16[416,256]{1,0:T(8,128)(2,1)S(1)} collective-permute-done((bf16[416,256]{1,0:T(8,128)(2,1)S(1)}, bf16[416,256]{1,0:T(8,128)(2,1)S(1)}, u32[]{:S(2)}, u32[]{:S(2)}) %collective-permute-start.5) | collective-permute-done | bytes 213024 | tf_op jit(solution)/shard_map/ppermute | solution.py:54
  67.1 3.2 %collective-permute-start.13 = (bf16[1664,256]{1,0:T(8,128)(2,1)}, bf16[1664,256]{1,0:T(8,128)(2,1)}, u32[]{:S(2)}, u32[]{:S(2)}) collective-permute-start(bf16[1664,256]{1,0:T(8,128)(2,1)} %constant_dynamic-update-slice_fusion.4), channel_id=1, source_target_pairs={{0,3},{1,0},{2,1},{3,2},{4,7},{5,4},{6,5},{7,6},{8,11},{9,8},{10,9... | collective-permute-start | bytes 2555912 | tf_op jit(solution)/shard_map/ppermute | solution.py:54
  75.3 3.9 %collective-permute-start.11 = (bf16[416,256]{1,0:T(8,128)(2,1)}, bf16[416,256]{1,0:T(8,128)(2,1)S(1)}, u32[]{:S(2)}, u32[]{:S(2)}) collective-permute-start(bf16[416,256]{1,0:T(8,128)(2,1)} %slice.77), channel_id=1, source_target_pairs={{0,12},{1,13},{2,14},{3,15},{4,0},{5,1},{6,2},{7,3},{8,4},{9,5},{1... | collective-permute-start | bytes 638984 | tf_op jit(solution)/shard_map/ppermute | solution.py:54
  80.1 25.5 %collective-permute-done.10.refs_7_ = bf16[416,256]{1,0:T(8,128)(2,1)S(1)} collective-permute-done((bf16[416,256]{1,0:T(8,128)(2,1)}, bf16[416,256]{1,0:T(8,128)(2,1)S(1)}, u32[]{:S(2)}, u32[]{:S(2)}) %collective-permute-start.10) | collective-permute-done | bytes 213024 | tf_op jit(solution)/shard_map/ppermute | solution.py:54
  108.1 3.2 %collective-permute-start.16 = (bf16[1664,256]{1,0:T(8,128)(2,1)S(1)}, bf16[1664,256]{1,0:T(8,128)(2,1)S(1)}, u32[]{:S(2)}, u32[]{:S(2)}) collective-permute-start(bf16[1664,256]{1,0:T(8,128)(2,1)S(1)} %get-tuple-element.79), channel_id=1, source_target_pairs={{0,3},{1,0},{2,1},{3,2},{4,7},{5,4},{6,5},{7,6},{8,11},{9,8},{10,9... | collective-permute-start | bytes 2555912 | tf_op jit(solution)/shard_map/ppermute | solution.py:54
  113.8 8.2 %shard_map.128.refs_1_ = bf16[4096,1024]{1,0:T(8,128)(2,1)} custom-call(s32[16]{0:T(128)S(1)} %fusion.13.slots, s32[8,16]{1,0:T(8,128)S(1)} %copy-done.9, s32[8]{0:T(128)S(1)} %copy-done.10, bf16[8,8,128,128]{3,2,1,0:T(8,128)(2,1)S(1)} %constant_dynamic-update-slice_fusion.mine, bf16[8,8,128,128]{3,2,1,0:T(8,128)(2,1)} %collective-permute-done.14.theirs), custom_call_target="tpu_custom_call" | custom-call | bytes 12582912 | tf_op jit(solution)/shard_map/pallas_call | solution.py:117
  122.1 9.4 %shard_map.129.refs_4_ = f32[832,1024]{1,0:T(8,128)} custom-call(s32[11]{0:T(128)S(1)} %fusion.14.refs_0_, bf16[4096,1024]{1,0:T(8,128)(2,1)} %shard_map.128.refs_1_, bf16[832,256]{1,0:T(8,128)(2,1)S(1)} %copy-done.11, bf16[832,256]{1,0:T(8,128)(2,1)S(1)} %collective-permute-done.1.refs_3_, bf16[832,256]{1,0:T(8,128)(2,1)S(1)} %collective-permute-done.2.refs_4_, ...), custom_call_target="tpu_custom_call" | custom-call | flops 4798283776 | bytes 17268736 | tf_op jit(solution)/shard_map/pallas_call | solution.py:219
  131.5 5.6 %collective-permute-done.15.refs_2_ = bf16[1664,256]{1,0:T(8,128)(2,1)S(1)} collective-permute-done((bf16[1664,256]{1,0:T(8,128)(2,1)S(1)}, bf16[1664,256]{1,0:T(8,128)(2,1)S(1)}, u32[]{:S(2)}, u32[]{:S(2)}) %collective-permute-start.15) | collective-permute-done | bytes 852000 | tf_op jit(solution)/shard_map/ppermute | solution.py:54
  137.5 3.3 %collective-permute-start.18 = (bf16[416,256]{1,0:T(8,128)(2,1)S(1)}, bf16[416,256]{1,0:T(8,128)(2,1)S(1)}, u32[]{:S(2)}, u32[]{:S(2)}) collective-permute-start(bf16[416,256]{1,0:T(8,128)(2,1)S(1)} %slice.81), channel_id=1, source_target_pairs={{0,3},{1,0},{2,1},{3,2},{4,7},{5,4},{6,5},{7,6},{8,11},{9,8},{10,9... | collective-permute-start | bytes 638984 | tf_op jit(solution)/shard_map/ppermute | solution.py:54
  140.7 6.8 %shard_map.130.refs_4_ = f32[832,1024]{1,0:T(8,128)} custom-call(s32[4]{0:T(128)S(1)} %fusion.15.refs_0_, bf16[4096,1024]{1,0:T(8,128)(2,1)} %shard_map.128.refs_1_, bf16[1664,256]{1,0:T(8,128)(2,1)S(1)} %collective-permute-done.15.refs_2_, bf16[1664,256]{1,0:T(8,128)(2,1)S(1)} %collective-permute-done.16.refs_3_, f32[832,1024]{1,0:T(8,128)} %shard_map.129.refs_4_), custom_call_target="tpu_custom_call" | custom-call | flops 1744830464 | bytes 10616832 | tf_op jit(solution)/shard_map/pallas_call | solution.py:219
  147.6 10.7 %shard_map.131.refs_7_ = bf16[1536,1024]{1,0:T(8,128)(2,1)} custom-call(s32[16]{0:T(128)S(1)} %iota.17.refs_0_, bf16[4096,1024]{1,0:T(8,128)(2,1)} %shard_map.128.refs_1_, bf16[16,704,256]{2,1,0:T(8,128)(2,1)} %bitcast.45, f32[1,1024]{1,0:T(1,128)S(1)} %bitcast.42, f32[704,1]{1,0:T(8,128)S(1)} %copy-done), custom_call_target="tpu_custom_call" | custom-call | flops 5905580032 | bytes 19922944 | tf_op jit(solution)/shard_map/pallas_call | solution.py:219
  158.3 4.6 %shard_map.132 = bf16[1536,1024]{1,0:T(8,128)(2,1)} custom-call(s32[1]{0:T(128)} %bitcast.refs_0_, bf16[4096,1024]{1,0:T(8,128)(2,1)} %shard_map.128.refs_1_, bf16[416,256]{1,0:T(8,128)(2,1)S(1)} %collective-permute-done.17.refs_2_, bf16[416,256]{1,0:T(8,128)(2,1)S(1)} %collective-permute-done.18.refs_3_, ...), custom_call_target="tpu_custom_call", output_to_operand_aliasing={{}: (7, {})} | custom-call | flops 436207616 | bytes 7766016 | tf_op jit(solution)/shard_map/pallas_call | solution.py:219
  (96 shorter events, 16.7 us)
Async XLA Ops:
  6.5 141.1 %all-gather.3.cloned.1.call-start = ((), (), s32[]{:S(2)}) async-start(), calls=%async_computation | async-start | bytes 6127616 | tf_op jit(solution)/shard_map/all_gather | solution.py:255
  10.1 8.3 %collective-permute-start = (bf16[8,1,128,128]{3,2,1,0:T(8,128)(2,1)}, bf16[8,1,128,128]{3,2,1,0:T(8,128)(2,1)S(1)}, u32[]{:S(2)}, u32[]{:S(2)}) collective-permute-start(bf16[8,1,128,128]{3,2,1,0:T(8,128)(2,1)} %param.19), channel_id=1, source_target_pairs={{0,32},{16,48},{32,0},{48,16},{64,96},{80,112},{96,64},{112,80},{1... | collective-permute-start | bytes 786440 | tf_op jit(solution)/shard_map/ppermute | solution.py:62
  19.5 14.6 %collective-permute-start.3 = (bf16[832,256]{1,0:T(8,128)(2,1)}, bf16[832,256]{1,0:T(8,128)(2,1)S(1)}, u32[]{:S(2)}, u32[]{:S(2)}) collective-permute-start(bf16[832,256]{1,0:T(8,128)(2,1)} %get-tuple-element.56.refs_2_), channel_id=1, source_target_pairs={{0,1},{1,2},{2,3},{3,0},{4,5},{5,6},{6,7},{7,4},{8,9},{9,10},{10,1... | collective-permute-start | bytes 1277960 | tf_op jit(solution)/shard_map/ppermute | solution.py:54
  21.0 16.2 %collective-permute-start.4 = (bf16[832,256]{1,0:T(8,128)(2,1)}, bf16[832,256]{1,0:T(8,128)(2,1)S(1)}, u32[]{:S(2)}, u32[]{:S(2)}) collective-permute-start(bf16[832,256]{1,0:T(8,128)(2,1)} %get-tuple-element.56.refs_2_), channel_id=1, source_target_pairs={{0,3},{1,0},{2,1},{3,2},{4,7},{5,4},{6,5},{7,6},{8,11},{9,8},{10,9... | collective-permute-start | bytes 1277960 | tf_op jit(solution)/shard_map/ppermute | solution.py:54
  22.8 34.5 %collective-permute-start.1 = (bf16[832,256]{1,0:T(8,128)(2,1)}, bf16[832,256]{1,0:T(8,128)(2,1)S(1)}, u32[]{:S(2)}, u32[]{:S(2)}) collective-permute-start(bf16[832,256]{1,0:T(8,128)(2,1)} %get-tuple-element.56.refs_2_), channel_id=1, source_target_pairs={{0,4},{1,5},{2,6},{3,7},{4,8},{5,9},{6,10},{7,11},{8,12},{9,13},{1... | collective-permute-start | bytes 1277960 | tf_op jit(solution)/shard_map/ppermute | solution.py:54
  26.0 31.2 %collective-permute-start.2 = (bf16[832,256]{1,0:T(8,128)(2,1)}, bf16[832,256]{1,0:T(8,128)(2,1)S(1)}, u32[]{:S(2)}, u32[]{:S(2)}) collective-permute-start(bf16[832,256]{1,0:T(8,128)(2,1)} %get-tuple-element.56.refs_2_), channel_id=1, source_target_pairs={{0,12},{1,13},{2,14},{3,15},{4,0},{5,1},{6,2},{7,3},{8,4},{9,5},{1... | collective-permute-start | bytes 1277960 | tf_op jit(solution)/shard_map/ppermute | solution.py:54
  28.2 32.5 %collective-permute-start.7 = (bf16[8,2,128,128]{3,2,1,0:T(8,128)(2,1)S(1)}, bf16[8,2,128,128]{3,2,1,0:T(8,128)(2,1)S(1)}, u32[]{:S(2)}, u32[]{:S(2)}) collective-permute-start(bf16[8,2,128,128]{3,2,1,0:T(8,128)(2,1)S(1)} %pad_maximum_fusion.4), channel_id=1, source_target_pairs={{0,64},{16,80},{32,96},{48,112},{64,128},{80,144},{96,160},{112,17... | collective-permute-start | bytes 1572872 | tf_op jit(solution)/shard_map/ppermute | solution.py:58
  34.1 23.2 %copy-start.5 = (bf16[832,256]{1,0:T(8,128)(2,1)}, bf16[832,256]{1,0:T(8,128)(2,1)S(1)}, u32[]{:S(2)}) copy-start(bf16[832,256]{1,0:T(8,128)(2,1)S(1)} %collective-permute-done.3.refs_5_) | copy-start | bytes 1277956
  34.1 26.6 %collective-permute-start.8 = (bf16[8,2,128,128]{3,2,1,0:T(8,128)(2,1)S(1)}, bf16[8,2,128,128]{3,2,1,0:T(8,128)(2,1)S(1)}, u32[]{:S(2)}, u32[]{:S(2)}) collective-permute-start(bf16[8,2,128,128]{3,2,1,0:T(8,128)(2,1)S(1)} %pad_maximum_fusion.4), channel_id=1, source_target_pairs={{0,128},{16,144},{32,160},{48,176},{64,192},{80,208},{96,224},{112... | collective-permute-start | bytes 1572872 | tf_op jit(solution)/shard_map/ppermute | solution.py:58
  37.3 20.0 %copy-start.7 = (bf16[832,256]{1,0:T(8,128)(2,1)}, bf16[832,256]{1,0:T(8,128)(2,1)S(1)}, u32[]{:S(2)}) copy-start(bf16[832,256]{1,0:T(8,128)(2,1)S(1)} %collective-permute-done.4.refs_6_) | copy-start | bytes 1277956
  37.3 23.4 %collective-permute-start.9 = (bf16[8,2,128,128]{3,2,1,0:T(8,128)(2,1)S(1)}, bf16[8,2,128,128]{3,2,1,0:T(8,128)(2,1)S(1)}, u32[]{:S(2)}, u32[]{:S(2)}) collective-permute-start(bf16[8,2,128,128]{3,2,1,0:T(8,128)(2,1)S(1)} %pad_maximum_fusion.4), channel_id=1, source_target_pairs={{0,192},{16,208},{32,224},{48,240},{64,0},{80,16},{96,32},{112,48}... | collective-permute-start | bytes 1572872 | tf_op jit(solution)/shard_map/ppermute | solution.py:58
  57.3 7.8 %collective-permute-start.5 = (bf16[416,256]{1,0:T(8,128)(2,1)S(1)}, bf16[416,256]{1,0:T(8,128)(2,1)S(1)}, u32[]{:S(2)}, u32[]{:S(2)}) collective-permute-start(bf16[416,256]{1,0:T(8,128)(2,1)S(1)} %slice.92), channel_id=1, source_target_pairs={{0,1},{1,2},{2,3},{3,0},{4,5},{5,6},{6,7},{7,4},{8,9},{9,10},{10,1... | collective-permute-start | bytes 638984 | tf_op jit(solution)/shard_map/ppermute | solution.py:54
  57.3 7.8 %collective-permute-start.6 = (bf16[416,256]{1,0:T(8,128)(2,1)S(1)}, bf16[416,256]{1,0:T(8,128)(2,1)S(1)}, u32[]{:S(2)}, u32[]{:S(2)}) collective-permute-start(bf16[416,256]{1,0:T(8,128)(2,1)S(1)} %slice.93), channel_id=1, source_target_pairs={{0,3},{1,0},{2,1},{3,2},{4,7},{5,4},{6,5},{7,6},{8,11},{9,8},{10,9... | collective-permute-start | bytes 638984 | tf_op jit(solution)/shard_map/ppermute | solution.py:54
  65.1 14.0 %copy-start.16 = (s32[2,1536]{1,0:T(2,128)S(1)}, s32[2,1536]{1,0:T(2,128)}, u32[]{:S(2)}) copy-start(s32[2,1536]{1,0:T(2,128)} %param.22) | copy-start | bytes 36868
  65.3 14.8 %copy-start.17 = (s32[2,1024]{1,0:T(2,128)S(1)}, s32[2,1024]{1,0:T(2,128)}, u32[]{:S(2)}) copy-start(s32[2,1024]{1,0:T(2,128)} %param.23) | copy-start | bytes 24580
  65.3 40.3 %collective-permute-start.14 = (bf16[8,8,128,128]{3,2,1,0:T(8,128)(2,1)S(1)}, bf16[8,8,128,128]{3,2,1,0:T(8,128)(2,1)}, u32[]{:S(2)}, u32[]{:S(2)}) collective-permute-start(bf16[8,8,128,128]{3,2,1,0:T(8,128)(2,1)S(1)} %constant_dynamic-update-slice_fusion.mine), channel_id=1, source_target_pairs={{0,16},{16,0},{32,48},{48,32},{64,80},{80,64},{96,112},{112,96},{1... | collective-permute-start | bytes 6291464 | tf_op jit(solution)/shard_map/ppermute | solution.py:62
  67.0 38.6 %collective-permute-start.12 = (bf16[1664,256]{1,0:T(8,128)(2,1)}, bf16[1664,256]{1,0:T(8,128)(2,1)}, u32[]{:S(2)}, u32[]{:S(2)}) collective-permute-start(bf16[1664,256]{1,0:T(8,128)(2,1)} %constant_dynamic-update-slice_fusion.4), channel_id=1, source_target_pairs={{0,1},{1,2},{2,3},{3,0},{4,5},{5,6},{6,7},{7,4},{8,9},{9,10},{10,1... | collective-permute-start | bytes 2555912 | tf_op jit(solution)/shard_map/ppermute | solution.py:54
  67.1 38.5 %collective-permute-start.13 = (bf16[1664,256]{1,0:T(8,128)(2,1)}, bf16[1664,256]{1,0:T(8,128)(2,1)}, u32[]{:S(2)}, u32[]{:S(2)}) collective-permute-start(bf16[1664,256]{1,0:T(8,128)(2,1)} %constant_dynamic-update-slice_fusion.4), channel_id=1, source_target_pairs={{0,3},{1,0},{2,1},{3,2},{4,7},{5,4},{6,5},{7,6},{8,11},{9,8},{10,9... | collective-permute-start | bytes 2555912 | tf_op jit(solution)/shard_map/ppermute | solution.py:54
  75.0 30.6 %collective-permute-start.10 = (bf16[416,256]{1,0:T(8,128)(2,1)}, bf16[416,256]{1,0:T(8,128)(2,1)S(1)}, u32[]{:S(2)}, u32[]{:S(2)}) collective-permute-start(bf16[416,256]{1,0:T(8,128)(2,1)} %slice.76), channel_id=1, source_target_pairs={{0,4},{1,5},{2,6},{3,7},{4,8},{5,9},{6,10},{7,11},{8,12},{9,13},{1... | collective-permute-start | bytes 638984 | tf_op jit(solution)/shard_map/ppermute | solution.py:54
  75.3 30.3 %collective-permute-start.11 = (bf16[416,256]{1,0:T(8,128)(2,1)}, bf16[416,256]{1,0:T(8,128)(2,1)S(1)}, u32[]{:S(2)}, u32[]{:S(2)}) collective-permute-start(bf16[416,256]{1,0:T(8,128)(2,1)} %slice.77), channel_id=1, source_target_pairs={{0,12},{1,13},{2,14},{3,15},{4,0},{5,1},{6,2},{7,3},{8,4},{9,5},{1... | collective-permute-start | bytes 638984 | tf_op jit(solution)/shard_map/ppermute | solution.py:54
  108.0 29.0 %collective-permute-start.15 = (bf16[1664,256]{1,0:T(8,128)(2,1)S(1)}, bf16[1664,256]{1,0:T(8,128)(2,1)S(1)}, u32[]{:S(2)}, u32[]{:S(2)}) collective-permute-start(bf16[1664,256]{1,0:T(8,128)(2,1)S(1)} %get-tuple-element.80), channel_id=1, source_target_pairs={{0,1},{1,2},{2,3},{3,0},{4,5},{5,6},{6,7},{7,4},{8,9},{9,10},{10,1... | collective-permute-start | bytes 2555912 | tf_op jit(solution)/shard_map/ppermute | solution.py:54
  108.1 28.9 %collective-permute-start.16 = (bf16[1664,256]{1,0:T(8,128)(2,1)S(1)}, bf16[1664,256]{1,0:T(8,128)(2,1)S(1)}, u32[]{:S(2)}, u32[]{:S(2)}) collective-permute-start(bf16[1664,256]{1,0:T(8,128)(2,1)S(1)} %get-tuple-element.79), channel_id=1, source_target_pairs={{0,3},{1,0},{2,1},{3,2},{4,7},{5,4},{6,5},{7,6},{8,11},{9,8},{10,9... | collective-permute-start | bytes 2555912 | tf_op jit(solution)/shard_map/ppermute | solution.py:54
  137.1 21.2 %collective-permute-start.17 = (bf16[416,256]{1,0:T(8,128)(2,1)S(1)}, bf16[416,256]{1,0:T(8,128)(2,1)S(1)}, u32[]{:S(2)}, u32[]{:S(2)}) collective-permute-start(bf16[416,256]{1,0:T(8,128)(2,1)S(1)} %slice.80), channel_id=1, source_target_pairs={{0,1},{1,2},{2,3},{3,0},{4,5},{5,6},{6,7},{7,4},{8,9},{9,10},{10,1... | collective-permute-start | bytes 638984 | tf_op jit(solution)/shard_map/ppermute | solution.py:54
  137.5 20.8 %collective-permute-start.18 = (bf16[416,256]{1,0:T(8,128)(2,1)S(1)}, bf16[416,256]{1,0:T(8,128)(2,1)S(1)}, u32[]{:S(2)}, u32[]{:S(2)}) collective-permute-start(bf16[416,256]{1,0:T(8,128)(2,1)S(1)} %slice.81), channel_id=1, source_target_pairs={{0,3},{1,0},{2,1},{3,2},{4,7},{5,4},{6,5},{7,6},{8,11},{9,8},{10,9... | collective-permute-start | bytes 638984 | tf_op jit(solution)/shard_map/ppermute | solution.py:54
  (16 other events, 106.9 us)
Sparse Core Ops, SparseCore 0:
  10.2 121.7 all-gather.2

commit v2 on v0

v2 whole, which is shorter than its diff:
```python
import functools

import jax
import jax.numpy as jnp
import numpy as np
from jax import lax
from jax.experimental import pallas as pl
from jax.experimental.pallas import tpu as pltpu
from jax.sharding import PartitionSpec as P

ANY = pl.BlockSpec(memory_space=pl.ANY)
SMEM = pl.BlockSpec(memory_space=pltpu.SMEM)
VMEM = pl.BlockSpec(memory_space=pltpu.VMEM)
EARLY_VMEM = 27 * 1024 * 1024
LATE_VMEM = 11 * 1024 * 1024
RING = 4
CROSS_ROWS = 320
GROUP = 4
ORDER = (
    [(2, 0), (2, 1), (2, 3)]
    + [(0, 0), (0, 1), (0, 3), (1, 0), (3, 0), (1, 1), (1, 3), (3, 1), (3, 3), (1, 2), (3, 2)]
    + [(0, 2), (2, 2)]
)
TAIL_SLOTS = (0, 1, 2, 15, 14)


def slot_table():
    table = np.zeros((16, 16), np.int32)
    for pair in range(16):
        y, zlo, core = pair // 4, pair // 2 % 2, pair % 2
        for local in range(16):
            far, swapped, near = local // 8, local // 4 % 2, local // 2 % 2
            other_y = (y + 2 * far) % 4 ^ near
            table[pair, local] = other_y * 4 + (zlo ^ local % 2) * 2 + (core ^ swapped)
    return table


def order_table():
    table = np.zeros((16, 16), np.int32)
    for virt in range(RING * RING):
        for place, (dz, dx) in enumerate(ORDER):
            table[virt, (virt // RING - dz) % RING * RING + (virt % RING - dx) % RING] = place
    return table


def barrier(*arrays):
    return lax.optimization_barrier(arrays)


def after(array, *first):
    return lax.optimization_barrier((array,) + first)[0]


def virt_shift(array, dz, dx):
    pairs = [
        (z * RING + x, (z + dz) % RING * RING + (x + dx) % RING)
        for z in range(RING)
        for x in range(RING)
    ]
    return lax.ppermute(array, "virt", pairs)


def pair_swap(array, bit):
    return lax.ppermute(array, "pair", [(i, i ^ bit) for i in range(16)])


def opposite_y(array):
    return lax.ppermute(array, "pair", [(i, (i + 8) % 16) for i in range(16)])


def table_lookup(table, index):
    rows = -(-table.shape[0] // 128)
    padded = jnp.zeros((rows * 128,), jnp.float32).at[: table.shape[0]].set(table).reshape(rows, 128)
    chosen = (index[:, None] // 128 == jnp.arange(rows, dtype=jnp.int32)[None, :]).astype(jnp.float32)
    lines = jnp.dot(chosen, padded, precision=lax.Precision.HIGHEST)
    lane = index[:, None] % 128 == jnp.arange(128, dtype=jnp.int32)[None, :]
    return jnp.sum(jnp.where(lane, lines, 0.0), axis=1)


def mask_kernel(whole, amp_map, amplitudes, masked, front):
    for tile in range(amp_map.shape[1]):
        for column in range(amp_map.shape[0]):
            keep = amp_map[column, tile].astype(jnp.float32).astype(jnp.bfloat16)
            block = (slice(tile * 128, tile * 128 + 128), slice(column * 128, column * 128 + 128))
            masked[block] = amplitudes[block] * keep
    front[...] = masked[:whole]


def mask(amplitudes, amp_map, whole):
    rows, columns = amplitudes.shape
    return pl.pallas_call(
        functools.partial(mask_kernel, whole),
        in_specs=[SMEM, VMEM],
        out_specs=[VMEM] * 2,
        out_shape=[jax.ShapeDtypeStruct((n, columns), jnp.bfloat16) for n in (rows, whole)],
    )(amp_map.T, amplitudes)


def pack_kernel(plan, count, *refs):
    sem = refs[-1]
    copies = []
    for target, parts in zip(refs[count:-1], plan):
        at = 0
        for source, first, size in parts:
            copies.append(
                pltpu.make_async_copy(
                    refs[source].at[pl.ds(first, size)], target.at[pl.ds(at, size)], sem.at[len(copies)]
                )
            )
            at += size
    for copy in copies:
        copy.start()
    for copy in copies:
        copy.wait()


def pack(*lists):
    arrays, plan, shapes = [], [], []
    for parts in lists:
        made = []
        for array, first, size in parts:
            known = [i for i, other in enumerate(arrays) if other is array]
            if not known:
                arrays.append(array)
            made.append((known[0] if known else len(arrays) - 1, first, size))
        plan.append(made)
        shapes.append((sum(size for _, _, size in parts),) + parts[0][0].shape[1:])
    return pl.pallas_call(
        functools.partial(pack_kernel, plan, len(arrays)),
        in_specs=[ANY] * len(arrays),
        out_specs=[VMEM] * len(shapes),
        out_shape=[jax.ShapeDtypeStruct(shape, jnp.bfloat16) for shape in shapes],
        scratch_shapes=[pltpu.SemaphoreType.DMA((sum(len(parts) for parts in plan),))],
        cost_estimate=pl.CostEstimate(
            flops=0, bytes_accessed=sum(2 * int(np.prod(shape)) for shape in shapes), transcendentals=0
        ),
    )(*arrays)


def segment_dot(held, arrived, weights, first_slot, count):
    product = None
    for group in range(0, count, GROUP):
        last = min(group + GROUP, count)
        for j in range(group, last):
            arrived(j)
        part = jnp.dot(
            held[:, group * 256 : last * 256],
            weights[(first_slot + group) * 256 : (first_slot + last) * 256, :],
            preferred_element_type=jnp.float32,
        )
        product = part if product is None else product + part
    return product


def start_blocks(plan, pieces, held, held_sem):
    for s, (_, rows, _, parts) in enumerate(plan):
        for j, (piece, first) in enumerate(parts):
            pltpu.make_async_copy(
                pieces[piece].at[pl.ds(first, rows)],
                held[s].at[:, pl.ds(j * 256, 256)],
                held_sem[s].at[j],
            ).start()


def block_waiter(held, sem):
    def wait(j):
        slot = held.at[:, pl.ds(j * 256, 256)]
        pltpu.make_async_copy(slot, slot, sem.at[j]).wait()

    return wait


def early_kernel(plan, tile_count, piece_count, where, cols, live, *refs):
    sources, refs = refs[:tile_count], refs[tile_count:]
    pieces = refs[:piece_count]
    total, tail, weights, tiles, tile_sem = refs[piece_count : piece_count + 5]
    rest = refs[piece_count + 5 :]
    held, held_sem = rest[: len(plan)], rest[len(plan) :]
    slots = tiles.shape[0]
    each = slots // tile_count
    loads = [
        pltpu.make_async_copy(source, tiles.at[pl.ds(i * each, each)], tile_sem.at[i])
        for i, source in enumerate(sources)
    ]
    for load in loads:
        load.start()
    start_blocks(plan, pieces, held, held_sem)
    weights[...] = jnp.zeros_like(weights)
    for load in loads:
        load.wait()
    for k in range(cols.shape[0]):

        def place(local, carry, k=k):
            slot = where[local]

            @pl.when(slot < live[k])
            def _():
                column = cols[k, slot]
                row = where[slots + column // 2] * 256 + column % 2 * 128
                weights[pl.ds(pl.multiple_of(row, 128), 128), k * 128 : k * 128 + 128] = tiles[local, k]

            return carry

        lax.fori_loop(0, slots, place, 0)
    for i, slot in enumerate(TAIL_SLOTS):
        tail[i * 256 : i * 256 + 256, :] = weights[slot * 256 : slot * 256 + 256, :]
    for s, (first_row, rows, first_slot, parts) in enumerate(plan):
        total[first_row : first_row + rows, :] = segment_dot(
            held[s], block_waiter(held[s], held_sem[s]), weights, first_slot, len(parts)
        )


def late_kernel(plan, piece_count, weights, total, virtual_sum, pair_energy, *refs):
    pieces = refs[:piece_count]
    out, staged, out_sem = refs[piece_count : piece_count + 3]
    rest = refs[piece_count + 3 :]
    held, held_sem = rest[: len(plan)], rest[len(plan) :]
    start_blocks(plan, pieces, held, held_sem)
    stores = []
    for s, (first_row, rows, first_slot, parts) in enumerate(plan):
        span = slice(first_row, first_row + rows)
        product = total[span, :] + segment_dot(
            held[s], block_waiter(held[s], held_sem[s]), weights, first_slot, len(parts)
        )
        staged[span, :] = (product / (virtual_sum[...] - pair_energy[span, :])).astype(jnp.bfloat16)
        store = pltpu.make_async_copy(
            staged.at[pl.ds(first_row, rows)], out.at[pl.ds(first_row, rows)], out_sem.at[s]
        )
        store.start()
        stores.append(store)
    for store in stores:
        store.wait()


def block_scratch(plan):
    held = [pltpu.VMEM((rows, len(parts) * 256), jnp.bfloat16) for _, rows, _, parts in plan]
    return held + [pltpu.SemaphoreType.DMA((len(parts),)) for _, _, _, parts in plan]


def cost(plan, columns, extra):
    work = sum(rows * len(parts) for _, rows, _, parts in plan)
    return pl.CostEstimate(flops=2 * work * 256 * columns, bytes_accessed=work * 512 + extra, transcendentals=0)


def early_matmul(where, cols, live, tiles, plan, pieces):
    columns = cols.shape[0] * 128
    all_rows = sum(rows for _, rows, _, _ in plan)
    return pl.pallas_call(
        functools.partial(early_kernel, plan, len(tiles), len(pieces)),
        in_specs=[SMEM] * 3 + [ANY] * (len(tiles) + len(pieces)),
        out_specs=[VMEM, VMEM],
        out_shape=[
            jax.ShapeDtypeStruct((all_rows, columns), jnp.float32),
            jax.ShapeDtypeStruct((len(TAIL_SLOTS) * 256, columns), jnp.bfloat16),
        ],
        scratch_shapes=[
            pltpu.VMEM((16 * 256, columns), jnp.bfloat16),
            pltpu.VMEM((16,) + tiles[0].shape[1:], jnp.bfloat16),
            pltpu.SemaphoreType.DMA((len(tiles),)),
        ]
        + block_scratch(plan),
        cost_estimate=cost(plan, columns, 16 * 2**20),
        compiler_params=pltpu.CompilerParams(vmem_limit_bytes=EARLY_VMEM),
    )(where, cols, live, *tiles, *pieces)


def late_matmul(weights, total, energies, plan, pieces):
    rows, columns = total.shape
    return pl.pallas_call(
        functools.partial(late_kernel, plan, len(pieces)),
        in_specs=[VMEM] * 4 + [ANY] * len(pieces),
        out_specs=ANY,
        out_shape=jax.ShapeDtypeStruct((rows, columns), jnp.bfloat16),
        scratch_shapes=[
            pltpu.VMEM((rows, columns), jnp.bfloat16),
            pltpu.SemaphoreType.DMA((len(plan),)),
        ]
        + block_scratch(plan),
        cost_estimate=cost(plan, columns, 12 * 2**20),
        compiler_params=pltpu.CompilerParams(vmem_limit_bytes=LATE_VMEM),
    )(weights, total, *energies, *pieces)


def per_device(
    amplitudes,
    amp_map,
    integral_tiles,
    integral_cols,
    live_slots,
    pair_orbitals,
    virtual_pairs,
    occupied_energy,
    virtual_energy,
):
    row_count = amplitudes.shape[0]
    cross = CROSS_ROWS
    part = (row_count - cross) // 2
    whole = row_count - cross
    own, front = mask(amplitudes, amp_map, whole)
    pair = lax.axis_index("pair")
    virt = lax.axis_index("virt")

    spots = np.concatenate(
        [np.repeat(slot_table(), RING * RING, axis=0), np.tile(order_table(), (16, 1))], axis=1
    )
    where = jnp.asarray(spots)[pair * (RING * RING) + virt]

    have = {(0, 0, "p"): (own, 0), (0, 0, "q"): (own, part), (0, 0, "b"): (own, whole)}
    size = {"p": part, "q": part, "b": cross}

    def cut(*lists):
        return pack(*[[have[key] + (size[key[2]],) for key in keys] for keys in lists])

    def arrive(array, keys, dz, dx):
        at = 0
        for z, x, s in keys:
            have[(z + dz) % RING, (x + dx) % RING, s] = (array, at)
            at += size[s]

    def send(array, dz, dx, keys):
        array = virt_shift(array, dz, dx)
        arrive(array, keys, dz, dx)
        return array

    def named(names, z, x):
        return [(z, x, s) for s in names]

    tiles = integral_tiles.reshape((1, integral_tiles.shape[0]) + integral_tiles.shape[2:])
    partner = pair_swap(tiles, 2)
    own, front, partner = barrier(own, front, partner)
    have.update({(0, 0, "p"): (own, 0), (0, 0, "q"): (own, part), (0, 0, "b"): (own, whole)})
    (two,) = pack([(tiles, 0, 1), (partner, 0, 1)])

    z1 = send(front, 1, 0, named("pq", 0, 0))
    z3 = send(front, -1, 0, named("pq", 0, 0))
    x1 = send(own, 0, 1, named("pqb", 0, 0))
    x3 = send(own, 0, -1, named("pqb", 0, 0))
    (four,) = pack([(two, 0, 2), (pair_swap(two, 4), 0, 2)])
    (cross,) = cut(named("b", 0, 1))
    x2 = send(cross, 0, 1, named("b", 0, 1))

    pair_orbitals, virtual_pairs = after(pair_orbitals, z1), after(virtual_pairs, z1)
    occupied = table_lookup(occupied_energy, pair_orbitals.reshape(-1)).reshape(2, -1)
    virtual = table_lookup(virtual_energy, virtual_pairs.reshape(-1)).reshape(2, -1)
    pair_energy = (occupied[0] + occupied[1])[:, None]
    virtual_sum = (virtual[0] + virtual[1])[None, :]
    near = named("pq", 1, 0) + named("pq", 3, 0)
    up_keys, down_keys = [(1, 0, "p"), (0, 0, "b")], [(3, 0, "q"), (0, 0, "b")]
    up, down, sides = cut(up_keys, down_keys, near)
    up, down, sides, four = barrier(up, down, sides, four, z1, z3, x1, x3, x2)[:4]
    far_four = opposite_y(four)
    z1 = send(up, 1, 0, up_keys)
    z3 = send(down, -1, 0, down_keys)
    x1 = send(sides, 0, 1, near)
    x3 = send(sides, 0, -1, near)
    crossing = named("b", 0, 1) + named("b", 0, 3) + named("b", 0, 2)
    (crossing_rows,) = cut(crossing)
    right_keys = named("pq", 2, 0) + named("pq", 1, 1)
    left_keys = named("pq", 2, 0) + named("pq", 3, 3)
    right, left = cut(right_keys, left_keys)
    crossing_rows, right, left, far_four, pair_energy, virtual_sum = barrier(
        crossing_rows, right, left, far_four, pair_energy, virtual_sum, z1, z3, x1, x3
    )[:6]
    far_other = pair_swap(far_four, 1)
    z1 = send(crossing_rows, 1, 0, crossing)
    z3 = send(crossing_rows, -1, 0, crossing)
    x1 = send(right, 0, 1, right_keys)
    x3 = send(left, 0, -1, left_keys)

    def planned(*segments):
        plan, pieces = [], []
        for segment, slot, names in segments:
            parts = []
            for name in names:
                array, at = have[name + (segment,)]
                known = [i for i, piece in enumerate(pieces) if piece is array]
                if not known:
                    pieces.append(array)
                parts.append((known[0] if known else len(pieces) - 1, at))
            start = {"p": 0, "q": part, "b": whole}[segment]
            plan.append((start, size[segment], slot, tuple(parts)))
        return tuple(plan), pieces

    up_keys, down_keys = [(1, 0, "b"), (1, 1, "b")], [(3, 3, "b"), (3, 2, "b")]
    right_keys, left_keys = [(2, 1, "p"), (0, 1, "p")], [(2, 3, "q"), (0, 3, "q")]
    up, down, right, left = cut(up_keys, down_keys, right_keys, left_keys)
    up, down, right, left, four, far_other = barrier(
        up, down, right, left, four, far_other, z1, z3, x1, x3
    )[:6]
    other_four = pair_swap(four, 1)
    send(up, 1, 0, up_keys)
    send(down, -1, 0, down_keys)
    send(right, 0, 1, right_keys)
    send(left, 0, -1, left_keys)

    total, tail = early_matmul(
        where,
        integral_cols,
        live_slots,
        [four, other_four, far_four, far_other],
        *planned(("p", 0, ORDER[:14]), ("q", 0, ORDER[:14]), ("b", 3, ORDER[3:15])),
    )
    last = [(2, 2), (0, 2)]
    return late_matmul(
        tail,
        total,
        (virtual_sum, pair_energy),
        *planned(("p", 3, last), ("q", 3, last), ("b", 0, [(2, 0), (2, 1), (2, 3), (2, 2)])),
    )


def solution(mesh):
    placed = (
        P("pair", "virt"),
        P("pair", "virt"),
        P("virt", "pair", None, None),
        P("virt", None),
        P("virt"),
        P(None, "pair"),
        P(None, "virt"),
        P(),
        P(),
    )
    return jax.shard_map(
        per_device, mesh=mesh, in_specs=placed, out_specs=P("pair", "virt"), check_vma=False
    )
```

time: 249 us -> 156 us (0.63)
  waiting for transfers between devices: 156 us -> 60.4 us
  Pallas kernels: 0 us -> 42.5 us
  starting transfers between devices: 0.04 us -> 37.5 us
  local copies, waits for them, and re-layouts: 42.5 us -> 9.61 us
  matrix products: 25.9 us -> 2.17 us
  between operations: 13.6 us -> 0.62 us
  other arithmetic: 5.48 us -> 0.03 us
    all_gather x2 -> x0, waiting for transfers between devices: 156 us -> none  [the longest x1 145 us: per_device(): lax.all_gather(masked, 'virt', axis=1, tiled=True)]
    ppermute x0 -> x22, waiting for transfers between devices: none -> 60.4 us  [the longest x17 56.3 us: virt_shift(): return lax.ppermute(array, 'virt', pairs)]
    pallas_call x0 -> x10, Pallas kernels: none -> 42.5 us  [the longest x1 19.4 us: early_matmul(): pl.pallas_call(functools.partial(early_kernel, plan, len(tiles), len(piec...]
    ppermute x0 -> x22, starting transfers between devices: none -> 37.5 us  [the longest x17 30.7 us: virt_shift(): return lax.ppermute(array, 'virt', pairs)]
    gather x4 -> x0, local copies, waits for them, and re-layouts: 29.1 us -> none  [the longest x1 8.39 us: pair_denominator(): jnp.take(occupied_energy, pair_orbitals[1])]
    dot_general x2, matrix products: 25.9 us -> 2.17 us  [table_lookup(): lines = jnp.dot(chosen, padded, precision=lax.Precision.HIGHEST)]
    convert_element_type x2 -> x0, local copies, waits for them, and re-layouts: 12.1 us -> none  [the longest x1 12 us: per_device(): dense_block.astype(jnp.bfloat16)]
    unnamed x10 -> x54, local copies, waits for them, and re-layouts: 0.03 us -> 8.6 us
  transfers between devices with their start and end apart: 2 -> 22, of which waited for: 2 -> 9; matrix products, arithmetic and copies ran while one was open for 22% -> 2% of each run, Pallas kernels for 0% -> 25%
where the time goes in v2:
time: 156 us; the launch traced here: 153 us
  waiting for transfers between devices  60.4 us (39%)
  Pallas kernels  42.5 us (27%)
  starting transfers between devices  37.5 us (24%)
  local copies, waits for them, and re-layouts  9.61 us (6%)
  matrix products  2.17 us (1%)
    ppermute x17, waiting for transfers between devices, virt_shift(): return lax.ppermute(array, 'virt', pairs)  56.3 us
    ppermute x17, starting transfers between devices, virt_shift(): return lax.ppermute(array, 'virt', pairs)  30.7 us
    pallas_call x1, Pallas kernels, early_matmul(): pl.pallas_call(functools.partial(early_kernel, plan, len(tiles), len(piec...  19.4 us
    pallas_call x7, Pallas kernels, pack(): pl.pallas_call(functools.partial(pack_kernel, plan, len(arrays)), in_spec...  16.6 us
    unnamed x54, local copies, waits for them, and re-layouts  8.6 us
    ppermute x4, waiting for transfers between devices, pair_swap(): return lax.ppermute(array, 'pair', [(i, i ^ bit) for i in range(16)])  4.07 us
    pallas_call x1, Pallas kernels, late_matmul(): pl.pallas_call(functools.partial(late_kernel, plan, len(pieces)), in_spec...  4.06 us
    ppermute x4, starting transfers between devices, pair_swap(): return lax.ppermute(array, 'pair', [(i, i ^ bit) for i in range(16)])  3.6 us
  transfers between devices with their start and end apart: 22, of which 9 were waited for; matrix products, arithmetic and copies ran while one was open for 2% of the time, Pallas kernels for 25%

profile of v2, /device:TPU:32, one launch (start us, length us, event | category | flops | bytes accessed | tf_op | source)
XLA Modules:
  0.0 152.8 jit_solution(12763263872425968732)
XLA Ops:
  1.8 2.4 %shard_map.100 = (bf16[1536,256]{1,0:T(8,128)(2,1)}, bf16[1216,256]{1,0:T(8,128)(2,1)}) custom-call(s32[2,12]{1,0:T(2,128)} %bitcast.42, bf16[1536,256]{1,0:T(8,128)(2,1)} %amplitudes.1), custom_call_target="tpu_custom_call" | custom-call | tf_op jit(solution)/shard_map/pallas_call | solution.py:91
  4.3 4.0 %collective-permute-done.refs_1_ = bf16[1,8,128,128]{3,2,1,0:T(8,128)(2,1)S(1)} collective-permute-done((bf16[1,8,128,128]{3,2,1,0:T(8,128)(2,1)}, bf16[1,8,128,128]{3,2,1,0:T(8,128)(2,1)S(1)}, u32[]{:S(2)}, u32[]{:S(2)}) %collective-permute-start) | collective-permute-done | bytes 262176 | tf_op jit(solution)/shard_map/ppermute | solution.py:64
  11.5 3.3 %collective-permute-start.1 = (bf16[1216,256]{1,0:T(8,128)(2,1)}, bf16[1216,256]{1,0:T(8,128)(2,1)S(1)}, u32[]{:S(2)}, u32[]{:S(2)}) collective-permute-start(bf16[1216,256]{1,0:T(8,128)(2,1)} %get-tuple-element.65), channel_id=1, source_target_pairs={{0,4},{1,5},{2,6},{3,7},{4,8},{5,9},{6,10},{7,11},{8,12},{9,13},{1... | collective-permute-start | bytes 1867784 | tf_op jit(solution)/shard_map/ppermute | solution.py:60
  14.8 2.1 %collective-permute-start.2 = (bf16[1216,256]{1,0:T(8,128)(2,1)}, bf16[1216,256]{1,0:T(8,128)(2,1)S(1)}, u32[]{:S(2)}, u32[]{:S(2)}) collective-permute-start(bf16[1216,256]{1,0:T(8,128)(2,1)} %get-tuple-element.65), channel_id=1, source_target_pairs={{0,12},{1,13},{2,14},{3,15},{4,0},{5,1},{6,2},{7,3},{8,4},{9,5},{1... | collective-permute-start | bytes 1867784 | tf_op jit(solution)/shard_map/ppermute | solution.py:60
  20.4 7.7 %collective-permute-done.4.refs_0_.refs_4_.refs_8_ = bf16[1536,256]{1,0:T(8,128)(2,1)S(1)} collective-permute-done((bf16[1536,256]{1,0:T(8,128)(2,1)}, bf16[1536,256]{1,0:T(8,128)(2,1)S(1)}, u32[]{:S(2)}, u32[]{:S(2)}) %collective-permute-start.4) | collective-permute-done | bytes 786464 | tf_op jit(solution)/shard_map/ppermute | solution.py:60
  31.8 2.2 %shard_map.103.refs_0_ = bf16[4,8,128,128]{3,2,1,0:T(8,128)(2,1)} custom-call(bf16[2,8,128,128]{3,2,1,0:T(8,128)(2,1)} %shard_map.102.refs_0_, bf16[2,8,128,128]{3,2,1,0:T(8,128)(2,1)} %copy-done.19), custom_call_target="tpu_custom_call" | custom-call | bytes 1048576 | tf_op jit(solution)/shard_map/pallas_call | solution.py:128
  34.0 9.0 %collective-permute-done.1.refs_0_.refs_10_ = bf16[1216,256]{1,0:T(8,128)(2,1)S(1)} collective-permute-done((bf16[1216,256]{1,0:T(8,128)(2,1)}, bf16[1216,256]{1,0:T(8,128)(2,1)S(1)}, u32[]{:S(2)}, u32[]{:S(2)}) %collective-permute-start.1) | collective-permute-done | bytes 622624 | tf_op jit(solution)/shard_map/ppermute | solution.py:60
  44.7 3.0 %shard_map.101 = (bf16[928,256]{1,0:T(8,128)(2,1)}, bf16[928,256]{1,0:T(8,128)(2,1)}, bf16[2432,256]{1,0:T(8,128)(2,1)}) custom-call(bf16[1216,256]{1,0:T(8,128)(2,1)} %copy-done.7, bf16[1536,256]{1,0:T(8,128)(2,1)} %get-tuple-element.66.refs_1_.refs_7_, bf16[1216,256]{1,0:T(8,128)(2,1)} %copy-done.9), custom_call_target="tpu_custom_call" | custom-call | bytes 2195456 | tf_op jit(solution)/shard_map/pallas_call | solution.py:128
  49.9 3.3 %collective-permute-start.11 = (bf16[4,8,128,128]{3,2,1,0:T(8,128)(2,1)}, bf16[4,8,128,128]{3,2,1,0:T(8,128)(2,1)}, u32[]{:S(2)}, u32[]{:S(2)}) collective-permute-start(bf16[4,8,128,128]{3,2,1,0:T(8,128)(2,1)} %shard_map.103.refs_0_), channel_id=1, source_target_pairs={{0,128},{16,144},{32,160},{48,176},{64,192},{80,208},{96,224},{112... | collective-permute-start | bytes 3145736 | tf_op jit(solution)/shard_map/ppermute | solution.py:68
  54.2 3.8 %collective-permute-start.7 = (bf16[928,256]{1,0:T(8,128)(2,1)S(1)}, bf16[928,256]{1,0:T(8,128)(2,1)S(1)}, u32[]{:S(2)}, u32[]{:S(2)}) collective-permute-start(bf16[928,256]{1,0:T(8,128)(2,1)S(1)} %copy-done.24), channel_id=1, source_target_pairs={{0,4},{1,5},{2,6},{3,7},{4,8},{5,9},{6,10},{7,11},{8,12},{9,13},{1... | collective-permute-start | bytes 1425416 | tf_op jit(solution)/shard_map/ppermute | solution.py:60
  59.7 1.9 %shard_map.105 = bf16[960,256]{1,0:T(8,128)(2,1)} custom-call(bf16[1536,256]{1,0:T(8,128)(2,1)} %copy-done, bf16[1536,256]{1,0:T(8,128)(2,1)} %copy-done.2, bf16[320,256]{1,0:T(8,128)(2,1)} %copy-done.15), custom_call_target="tpu_custom_call" | custom-call | bytes 491520 | tf_op jit(solution)/shard_map/pallas_call | solution.py:128
  61.6 9.7 %collective-permute-done.7.refs_0_.refs_4_ = bf16[928,256]{1,0:T(8,128)(2,1)S(1)} collective-permute-done((bf16[928,256]{1,0:T(8,128)(2,1)S(1)}, bf16[928,256]{1,0:T(8,128)(2,1)S(1)}, u32[]{:S(2)}, u32[]{:S(2)}) %collective-permute-start.7) | collective-permute-done | bytes 475168 | tf_op jit(solution)/shard_map/ppermute | solution.py:60
  71.3 5.9 %collective-permute-done.8.refs_1_.refs_14_ = bf16[928,256]{1,0:T(8,128)(2,1)S(1)} collective-permute-done((bf16[928,256]{1,0:T(8,128)(2,1)S(1)}, bf16[928,256]{1,0:T(8,128)(2,1)S(1)}, u32[]{:S(2)}, u32[]{:S(2)}) %collective-permute-start.8) | collective-permute-done | bytes 475168 | tf_op jit(solution)/shard_map/ppermute | solution.py:60
  77.3 2.1 %collective-permute-done.9.refs_2_.refs_12_ = bf16[2432,256]{1,0:T(8,128)(2,1)} collective-permute-done((bf16[2432,256]{1,0:T(8,128)(2,1)}, bf16[2432,256]{1,0:T(8,128)(2,1)}, u32[]{:S(2)}, u32[]{:S(2)}) %collective-permute-start.9) | collective-permute-done | bytes 1245216 | tf_op jit(solution)/shard_map/ppermute | solution.py:60
  79.4 3.1 %shard_map.106 = (bf16[2432,256]{1,0:T(8,128)(2,1)}, bf16[2432,256]{1,0:T(8,128)(2,1)}) custom-call(bf16[928,256]{1,0:T(8,128)(2,1)} %copy-done.4, bf16[928,256]{1,0:T(8,128)(2,1)} %copy-done.13, bf16[2432,256]{1,0:T(8,128)(2,1)} %collective-permute-done.9.refs_2_.refs_12_, bf16[2432,256]{1,0:T(8,128)(2,1)} %collective-permute-done.10.refs_3_.refs_13_), custom_call_target="tpu_custom_call" | custom-call | bytes 2490368 | tf_op jit(solution)/shard_map/pallas_call | solution.py:128
  82.7 3.2 %collective-permute-start.15 = (bf16[2432,256]{1,0:T(8,128)(2,1)}, bf16[2432,256]{1,0:T(8,128)(2,1)}, u32[]{:S(2)}, u32[]{:S(2)}) collective-permute-start(bf16[2432,256]{1,0:T(8,128)(2,1)} %get-tuple-element.81), channel_id=1, source_target_pairs={{0,3},{1,0},{2,1},{3,2},{4,7},{5,4},{6,5},{7,6},{8,11},{9,8},{10,9... | collective-permute-start | bytes 3735560 | tf_op jit(solution)/shard_map/ppermute | solution.py:60
  86.3 3.7 %collective-permute-start.13 = (bf16[960,256]{1,0:T(8,128)(2,1)}, bf16[960,256]{1,0:T(8,128)(2,1)}, u32[]{:S(2)}, u32[]{:S(2)}) collective-permute-start(bf16[960,256]{1,0:T(8,128)(2,1)} %shard_map.105), channel_id=1, source_target_pairs={{0,12},{1,13},{2,14},{3,15},{4,0},{5,1},{6,2},{7,3},{8,4},{9,5},{1... | collective-permute-start | bytes 1474568 | tf_op jit(solution)/shard_map/ppermute | solution.py:60
  90.1 16.4 %collective-permute-done.12.refs_1_.refs_15_ = bf16[960,256]{1,0:T(8,128)(2,1)S(1)} collective-permute-done((bf16[960,256]{1,0:T(8,128)(2,1)}, bf16[960,256]{1,0:T(8,128)(2,1)S(1)}, u32[]{:S(2)}, u32[]{:S(2)}) %collective-permute-start.12) | collective-permute-done | bytes 491552 | tf_op jit(solution)/shard_map/ppermute | solution.py:60
  106.4 5.5 %collective-permute-done.13.refs_2_.refs_16_ = bf16[960,256]{1,0:T(8,128)(2,1)} collective-permute-done((bf16[960,256]{1,0:T(8,128)(2,1)}, bf16[960,256]{1,0:T(8,128)(2,1)}, u32[]{:S(2)}, u32[]{:S(2)}) %collective-permute-start.13) | collective-permute-done | bytes 491552 | tf_op jit(solution)/shard_map/ppermute | solution.py:60
  111.9 2.9 %shard_map.107 = (bf16[640,256]{1,0:T(8,128)(2,1)}, bf16[640,256]{1,0:T(8,128)(2,1)}, bf16[1216,256]{1,0:T(8,128)(2,1)}, bf16[1216,256]{1,0:T(8,128)(2,1)}) custom-call(bf16[928,256]{1,0:T(8,128)(2,1)} %copy-done.4, bf16[960,256]{1,0:T(8,128)(2,1)} %copy-done.11, bf16[960,256]{1,0:T(8,128)(2,1)} %collective-permute-done.13.refs_2_.refs_16_, ...), custom_call_target="tpu_custom_call" | custom-call | bytes 1900544 | tf_op jit(solution)/shard_map/pallas_call | solution.py:128
  116.0 3.2 %collective-permute-start.19 = (bf16[1216,256]{1,0:T(8,128)(2,1)}, bf16[1216,256]{1,0:T(8,128)(2,1)S(1)}, u32[]{:S(2)}, u32[]{:S(2)}) collective-permute-start(bf16[1216,256]{1,0:T(8,128)(2,1)} %get-tuple-element.94), channel_id=1, source_target_pairs={{0,3},{1,0},{2,1},{3,2},{4,7},{5,4},{6,5},{7,6},{8,11},{9,8},{10,9... | collective-permute-start | bytes 1867784 | tf_op jit(solution)/shard_map/ppermute | solution.py:60
  119.3 3.7 %collective-permute-start.20 = (bf16[640,256]{1,0:T(8,128)(2,1)}, bf16[640,256]{1,0:T(8,128)(2,1)S(1)}, u32[]{:S(2)}, u32[]{:S(2)}) collective-permute-start(bf16[640,256]{1,0:T(8,128)(2,1)} %get-tuple-element.95), channel_id=1, source_target_pairs={{0,4},{1,5},{2,6},{3,7},{4,8},{5,9},{6,10},{7,11},{8,12},{9,13},{1... | collective-permute-start | bytes 983048 | tf_op jit(solution)/shard_map/ppermute | solution.py:60
  129.1 19.4 %shard_map.108 = (f32[1536,1024]{1,0:T(8,128)S(1)}, bf16[1280,1024]{1,0:T(8,128)(2,1)S(1)}) custom-call(s32[32]{0:T(128)S(1)} %dynamic-slice_bitcast_fusion.where, s32[8,16]{1,0:T(8,128)S(1)} %copy-done.17, s32[8]{0:T(128)S(1)} %copy-done.18, bf16[4,8,128,128]{3,2,1,0:T(8,128)(2,1)} %shard_map.103.refs_0_, ...), custom_call_target="tpu_custom_call" | custom-call | flops 10938744832 | bytes 27459584 | tf_op jit(solution)/shard_map/pallas_call | solution.py:248
  148.6 4.1 %shard_map.109 = bf16[1536,1024]{1,0:T(8,128)(2,1)} custom-call(bf16[1280,1024]{1,0:T(8,128)(2,1)S(1)} %get-tuple-element.89.weights, f32[1536,1024]{1,0:T(8,128)S(1)} %get-tuple-element.90.total, f32[1,1024]{1,0:T(1,128)S(1)} %bitcast.38, f32[1536,1]{1,0:T(8,128)S(1)} %copy.12.pair_energy, bf16[1216,256]{1,0:T(8,128)(2,1)S(1)} %collective-permute-done.18.refs_0_, ...), custom_call_target="tpu_custom_call" | custom-call | flops 1946157056 | bytes 14483456 | tf_op jit(solution)/shard_map/pallas_call | solution.py:269
  (94 shorter events, 26.5 us)
Async XLA Ops:
  0.0 8.3 %collective-permute-start = (bf16[1,8,128,128]{3,2,1,0:T(8,128)(2,1)}, bf16[1,8,128,128]{3,2,1,0:T(8,128)(2,1)S(1)}, u32[]{:S(2)}, u32[]{:S(2)}) collective-permute-start(bf16[1,8,128,128]{3,2,1,0:T(8,128)(2,1)} %bitcast.39), channel_id=1, source_target_pairs={{0,32},{16,48},{32,0},{48,16},{64,96},{80,112},{96,64},{112,80},{1... | collective-permute-start | bytes 786440 | tf_op jit(solution)/shard_map/ppermute | solution.py:64
  8.3 19.8 %collective-permute-start.4 = (bf16[1536,256]{1,0:T(8,128)(2,1)}, bf16[1536,256]{1,0:T(8,128)(2,1)S(1)}, u32[]{:S(2)}, u32[]{:S(2)}) collective-permute-start(bf16[1536,256]{1,0:T(8,128)(2,1)} %get-tuple-element.66.refs_1_.refs_7_), channel_id=1, source_target_pairs={{0,1},{1,2},{2,3},{3,0},{4,5},{5,6},{6,7},{7,4},{8,9},{9,10},{10,1... | collective-permute-start | bytes 2359304 | tf_op jit(solution)/shard_map/ppermute | solution.py:60
  9.8 38.0 %collective-permute-start.5 = (bf16[1536,256]{1,0:T(8,128)(2,1)}, bf16[1536,256]{1,0:T(8,128)(2,1)S(1)}, u32[]{:S(2)}, u32[]{:S(2)}) collective-permute-start(bf16[1536,256]{1,0:T(8,128)(2,1)} %get-tuple-element.66.refs_1_.refs_7_), channel_id=1, source_target_pairs={{0,3},{1,0},{2,1},{3,2},{4,7},{5,4},{6,5},{7,6},{8,11},{9,8},{10,9... | collective-permute-start | bytes 2359304 | tf_op jit(solution)/shard_map/ppermute | solution.py:60
  11.5 31.5 %collective-permute-start.1 = (bf16[1216,256]{1,0:T(8,128)(2,1)}, bf16[1216,256]{1,0:T(8,128)(2,1)S(1)}, u32[]{:S(2)}, u32[]{:S(2)}) collective-permute-start(bf16[1216,256]{1,0:T(8,128)(2,1)} %get-tuple-element.65), channel_id=1, source_target_pairs={{0,4},{1,5},{2,6},{3,7},{4,8},{5,9},{6,10},{7,11},{8,12},{9,13},{1... | collective-permute-start | bytes 1867784 | tf_op jit(solution)/shard_map/ppermute | solution.py:60
  14.8 28.3 %collective-permute-start.2 = (bf16[1216,256]{1,0:T(8,128)(2,1)}, bf16[1216,256]{1,0:T(8,128)(2,1)S(1)}, u32[]{:S(2)}, u32[]{:S(2)}) collective-permute-start(bf16[1216,256]{1,0:T(8,128)(2,1)} %get-tuple-element.65), channel_id=1, source_target_pairs={{0,12},{1,13},{2,14},{3,15},{4,0},{5,1},{6,2},{7,3},{8,4},{9,5},{1... | collective-permute-start | bytes 1867784 | tf_op jit(solution)/shard_map/ppermute | solution.py:60
  18.8 12.2 %collective-permute-start.3 = (bf16[2,8,128,128]{3,2,1,0:T(8,128)(2,1)}, bf16[2,8,128,128]{3,2,1,0:T(8,128)(2,1)S(1)}, u32[]{:S(2)}, u32[]{:S(2)}) collective-permute-start(bf16[2,8,128,128]{3,2,1,0:T(8,128)(2,1)} %shard_map.102.refs_0_), channel_id=1, source_target_pairs={{0,64},{16,80},{32,96},{48,112},{64,0},{80,16},{96,32},{112,48},{1... | collective-permute-start | bytes 1572872 | tf_op jit(solution)/shard_map/ppermute | solution.py:64
  30.6 17.2 %collective-permute-start.6 = (bf16[320,256]{1,0:T(8,128)(2,1)}, bf16[320,256]{1,0:T(8,128)(2,1)S(1)}, u32[]{:S(2)}, u32[]{:S(2)}) collective-permute-start(bf16[320,256]{1,0:T(8,128)(2,1)} %shard_map.104), channel_id=1, source_target_pairs={{0,1},{1,2},{2,3},{3,0},{4,5},{5,6},{6,7},{7,4},{8,9},{9,10},{10,1... | collective-permute-start | bytes 491528 | tf_op jit(solution)/shard_map/ppermute | solution.py:60
  47.8 29.5 %collective-permute-start.10 = (bf16[2432,256]{1,0:T(8,128)(2,1)}, bf16[2432,256]{1,0:T(8,128)(2,1)}, u32[]{:S(2)}, u32[]{:S(2)}) collective-permute-start(bf16[2432,256]{1,0:T(8,128)(2,1)} %get-tuple-element.73), channel_id=1, source_target_pairs={{0,3},{1,0},{2,1},{3,2},{4,7},{5,4},{6,5},{7,6},{8,11},{9,8},{10,9... | collective-permute-start | bytes 3735560 | tf_op jit(solution)/shard_map/ppermute | solution.py:60
  49.4 30.0 %collective-permute-start.9 = (bf16[2432,256]{1,0:T(8,128)(2,1)}, bf16[2432,256]{1,0:T(8,128)(2,1)}, u32[]{:S(2)}, u32[]{:S(2)}) collective-permute-start(bf16[2432,256]{1,0:T(8,128)(2,1)} %get-tuple-element.73), channel_id=1, source_target_pairs={{0,1},{1,2},{2,3},{3,0},{4,5},{5,6},{6,7},{7,4},{8,9},{9,10},{10,1... | collective-permute-start | bytes 3735560 | tf_op jit(solution)/shard_map/ppermute | solution.py:60
  49.9 32.6 %collective-permute-start.11 = (bf16[4,8,128,128]{3,2,1,0:T(8,128)(2,1)}, bf16[4,8,128,128]{3,2,1,0:T(8,128)(2,1)}, u32[]{:S(2)}, u32[]{:S(2)}) collective-permute-start(bf16[4,8,128,128]{3,2,1,0:T(8,128)(2,1)} %shard_map.103.refs_0_), channel_id=1, source_target_pairs={{0,128},{16,144},{32,160},{48,176},{64,192},{80,208},{96,224},{112... | collective-permute-start | bytes 3145736 | tf_op jit(solution)/shard_map/ppermute | solution.py:68
  54.2 17.1 %collective-permute-start.7 = (bf16[928,256]{1,0:T(8,128)(2,1)S(1)}, bf16[928,256]{1,0:T(8,128)(2,1)S(1)}, u32[]{:S(2)}, u32[]{:S(2)}) collective-permute-start(bf16[928,256]{1,0:T(8,128)(2,1)S(1)} %copy-done.24), channel_id=1, source_target_pairs={{0,4},{1,5},{2,6},{3,7},{4,8},{5,9},{6,10},{7,11},{8,12},{9,13},{1... | collective-permute-start | bytes 1425416 | tf_op jit(solution)/shard_map/ppermute | solution.py:60
  58.0 19.3 %collective-permute-start.8 = (bf16[928,256]{1,0:T(8,128)(2,1)S(1)}, bf16[928,256]{1,0:T(8,128)(2,1)S(1)}, u32[]{:S(2)}, u32[]{:S(2)}) collective-permute-start(bf16[928,256]{1,0:T(8,128)(2,1)S(1)} %copy-done.23), channel_id=1, source_target_pairs={{0,12},{1,13},{2,14},{3,15},{4,0},{5,1},{6,2},{7,3},{8,4},{9,5},{1... | collective-permute-start | bytes 1425416 | tf_op jit(solution)/shard_map/ppermute | solution.py:60
  82.5 41.3 %copy-start.1 = (bf16[1536,256]{1,0:T(8,128)(2,1)S(1)}, bf16[1536,256]{1,0:T(8,128)(2,1)}, u32[]{:S(2)}) copy-start(bf16[1536,256]{1,0:T(8,128)(2,1)} %copy-done) | copy-start | bytes 2359300
  82.6 41.3 %copy-start.3 = (bf16[1536,256]{1,0:T(8,128)(2,1)S(1)}, bf16[1536,256]{1,0:T(8,128)(2,1)}, u32[]{:S(2)}) copy-start(bf16[1536,256]{1,0:T(8,128)(2,1)} %copy-done.2) | copy-start | bytes 2359300
  82.6 29.3 %collective-permute-start.14 = (bf16[2432,256]{1,0:T(8,128)(2,1)}, bf16[2432,256]{1,0:T(8,128)(2,1)}, u32[]{:S(2)}, u32[]{:S(2)}) collective-permute-start(bf16[2432,256]{1,0:T(8,128)(2,1)} %get-tuple-element.80), channel_id=1, source_target_pairs={{0,1},{1,2},{2,3},{3,0},{4,5},{5,6},{6,7},{7,4},{8,9},{9,10},{10,1... | collective-permute-start | bytes 3735560 | tf_op jit(solution)/shard_map/ppermute | solution.py:60
  82.7 29.2 %collective-permute-start.15 = (bf16[2432,256]{1,0:T(8,128)(2,1)}, bf16[2432,256]{1,0:T(8,128)(2,1)}, u32[]{:S(2)}, u32[]{:S(2)}) collective-permute-start(bf16[2432,256]{1,0:T(8,128)(2,1)} %get-tuple-element.81), channel_id=1, source_target_pairs={{0,3},{1,0},{2,1},{3,2},{4,7},{5,4},{6,5},{7,6},{8,11},{9,8},{10,9... | collective-permute-start | bytes 3735560 | tf_op jit(solution)/shard_map/ppermute | solution.py:60
  85.9 28.9 %collective-permute-start.16 = (bf16[4,8,128,128]{3,2,1,0:T(8,128)(2,1)}, bf16[4,8,128,128]{3,2,1,0:T(8,128)(2,1)}, u32[]{:S(2)}, u32[]{:S(2)}) collective-permute-start(bf16[4,8,128,128]{3,2,1,0:T(8,128)(2,1)} %collective-permute-done.11.refs_2_), channel_id=1, source_target_pairs={{0,16},{16,0},{32,48},{48,32},{64,80},{80,64},{96,112},{112,96},{1... | collective-permute-start | bytes 3145736 | tf_op jit(solution)/shard_map/ppermute | solution.py:64
  85.9 20.5 %collective-permute-start.12 = (bf16[960,256]{1,0:T(8,128)(2,1)}, bf16[960,256]{1,0:T(8,128)(2,1)S(1)}, u32[]{:S(2)}, u32[]{:S(2)}) collective-permute-start(bf16[960,256]{1,0:T(8,128)(2,1)} %shard_map.105), channel_id=1, source_target_pairs={{0,4},{1,5},{2,6},{3,7},{4,8},{5,9},{6,10},{7,11},{8,12},{9,13},{1... | collective-permute-start | bytes 1474568 | tf_op jit(solution)/shard_map/ppermute | solution.py:60
  86.3 25.5 %collective-permute-start.13 = (bf16[960,256]{1,0:T(8,128)(2,1)}, bf16[960,256]{1,0:T(8,128)(2,1)}, u32[]{:S(2)}, u32[]{:S(2)}) collective-permute-start(bf16[960,256]{1,0:T(8,128)(2,1)} %shard_map.105), channel_id=1, source_target_pairs={{0,12},{1,13},{2,14},{3,15},{4,0},{5,1},{6,2},{7,3},{8,4},{9,5},{1... | collective-permute-start | bytes 1474568 | tf_op jit(solution)/shard_map/ppermute | solution.py:60
  114.8 9.0 %collective-permute-start.17 = (bf16[4,8,128,128]{3,2,1,0:T(8,128)(2,1)}, bf16[4,8,128,128]{3,2,1,0:T(8,128)(2,1)}, u32[]{:S(2)}, u32[]{:S(2)}) collective-permute-start(bf16[4,8,128,128]{3,2,1,0:T(8,128)(2,1)} %shard_map.103.refs_0_), channel_id=1, source_target_pairs={{0,16},{16,0},{32,48},{48,32},{64,80},{80,64},{96,112},{112,96},{1... | collective-permute-start | bytes 3145736 | tf_op jit(solution)/shard_map/ppermute | solution.py:64
  115.9 32.6 %collective-permute-start.18 = (bf16[1216,256]{1,0:T(8,128)(2,1)}, bf16[1216,256]{1,0:T(8,128)(2,1)S(1)}, u32[]{:S(2)}, u32[]{:S(2)}) collective-permute-start(bf16[1216,256]{1,0:T(8,128)(2,1)} %get-tuple-element.93), channel_id=1, source_target_pairs={{0,1},{1,2},{2,3},{3,0},{4,5},{5,6},{6,7},{7,4},{8,9},{9,10},{10,1... | collective-permute-start | bytes 1867784 | tf_op jit(solution)/shard_map/ppermute | solution.py:60
  116.0 32.5 %collective-permute-start.19 = (bf16[1216,256]{1,0:T(8,128)(2,1)}, bf16[1216,256]{1,0:T(8,128)(2,1)S(1)}, u32[]{:S(2)}, u32[]{:S(2)}) collective-permute-start(bf16[1216,256]{1,0:T(8,128)(2,1)} %get-tuple-element.94), channel_id=1, source_target_pairs={{0,3},{1,0},{2,1},{3,2},{4,7},{5,4},{6,5},{7,6},{8,11},{9,8},{10,9... | collective-permute-start | bytes 1867784 | tf_op jit(solution)/shard_map/ppermute | solution.py:60
  119.3 29.3 %collective-permute-start.20 = (bf16[640,256]{1,0:T(8,128)(2,1)}, bf16[640,256]{1,0:T(8,128)(2,1)S(1)}, u32[]{:S(2)}, u32[]{:S(2)}) collective-permute-start(bf16[640,256]{1,0:T(8,128)(2,1)} %get-tuple-element.95), channel_id=1, source_target_pairs={{0,4},{1,5},{2,6},{3,7},{4,8},{5,9},{6,10},{7,11},{8,12},{9,13},{1... | collective-permute-start | bytes 983048 | tf_op jit(solution)/shard_map/ppermute | solution.py:60
  123.0 25.6 %collective-permute-start.21 = (bf16[640,256]{1,0:T(8,128)(2,1)}, bf16[640,256]{1,0:T(8,128)(2,1)S(1)}, u32[]{:S(2)}, u32[]{:S(2)}) collective-permute-start(bf16[640,256]{1,0:T(8,128)(2,1)} %get-tuple-element.96), channel_id=1, source_target_pairs={{0,12},{1,13},{2,14},{3,15},{4,0},{5,1},{6,2},{7,3},{8,4},{9,5},{1... | collective-permute-start | bytes 983048 | tf_op jit(solution)/shard_map/ppermute | solution.py:60
  (25 other events, 321.7 us)

commit v3 on v2

--- a/solution.py
+++ b/solution.py
@@ -11,11 +11,11 @@
 ANY = pl.BlockSpec(memory_space=pl.ANY)
 SMEM = pl.BlockSpec(memory_space=pltpu.SMEM)
 VMEM = pl.BlockSpec(memory_space=pltpu.VMEM)
-EARLY_VMEM = 27 * 1024 * 1024
-LATE_VMEM = 11 * 1024 * 1024
+EARLY_VMEM = 30 * 1024 * 1024
+LATE_VMEM = 16 * 1024 * 1024
 RING = 4
 CROSS_ROWS = 320
-GROUP = 4
+GROUP = 5
 ORDER = (
     [(2, 0), (2, 1), (2, 3)]
     + [(0, 0), (0, 1), (0, 3), (1, 0), (3, 0), (1, 1), (1, 3), (3, 1), (3, 3), (1, 2), (3, 2)]
@@ -137,8 +137,7 @@
     )(*arrays)
 
 
-def segment_dot(held, arrived, weights, first_slot, count):
-    product = None
+def segment_dot(held, arrived, weights, first_slot, count, target):
     for group in range(0, count, GROUP):
         last = min(group + GROUP, count)
         for j in range(group, last):
@@ -148,18 +147,18 @@
             weights[(first_slot + group) * 256 : (first_slot + last) * 256, :],
             preferred_element_type=jnp.float32,
         )
-        product = part if product is None else product + part
-    return product
+        target[...] = part if group == 0 else target[...] + part
 
 
 def start_blocks(plan, pieces, held, held_sem):
-    for s, (_, rows, _, parts) in enumerate(plan):
-        for j, (piece, first) in enumerate(parts):
-            pltpu.make_async_copy(
-                pieces[piece].at[pl.ds(first, rows)],
-                held[s].at[:, pl.ds(j * 256, 256)],
-                held_sem[s].at[j],
-            ).start()
+    for s, (_, _, _, parts) in enumerate(plan):
+        for j, copies in enumerate(parts):
+            for piece, first, start, count in copies:
+                pltpu.make_async_copy(
+                    pieces[piece].at[pl.ds(first, count)],
+                    held[s].at[pl.ds(start, count), pl.ds(j * 256, 256)],
+                    held_sem[s].at[j],
+                ).start()
 
 
 def block_waiter(held, sem):
@@ -205,8 +204,9 @@
     for i, slot in enumerate(TAIL_SLOTS):
         tail[i * 256 : i * 256 + 256, :] = weights[slot * 256 : slot * 256 + 256, :]
     for s, (first_row, rows, first_slot, parts) in enumerate(plan):
-        total[first_row : first_row + rows, :] = segment_dot(
-            held[s], block_waiter(held[s], held_sem[s]), weights, first_slot, len(parts)
+        target = total.at[pl.ds(first_row, rows)]
+        segment_dot(
+            held[s], block_waiter(held[s], held_sem[s]), weights, first_slot, len(parts), target
         )
 
 
@@ -219,8 +219,13 @@
     stores = []
     for s, (first_row, rows, first_slot, parts) in enumerate(plan):
         span = slice(first_row, first_row + rows)
-        product = total[span, :] + segment_dot(
-            held[s], block_waiter(held[s], held_sem[s]), weights, first_slot, len(parts)
+        count = len(parts)
+        for j in range(count):
+            block_waiter(held[s], held_sem[s])(j)
+        product = total[span, :] + jnp.dot(
+            held[s][...],
+            weights[first_slot * 256 : (first_slot + count) * 256, :],
+            preferred_element_type=jnp.float32,
         )
         staged[span, :] = (product / (virtual_sum[...] - pair_energy[span, :])).astype(jnp.bfloat16)
         store = pltpu.make_async_copy(
@@ -369,16 +374,25 @@
 
     def planned(*segments):
         plan, pieces = [], []
-        for segment, slot, names in segments:
+        begin = {"p": 0, "q": part, "b": whole}
+        for letters, slot, names in segments:
             parts = []
             for name in names:
-                array, at = have[name + (segment,)]
-                known = [i for i, piece in enumerate(pieces) if piece is array]
-                if not known:
-                    pieces.append(array)
-                parts.append((known[0] if known else len(pieces) - 1, at))
-            start = {"p": 0, "q": part, "b": whole}[segment]
-            plan.append((start, size[segment], slot, tuple(parts)))
+                copies = []
+                for letter in letters:
+                    array, at = have[name + (letter,)]
+                    known = [i for i, piece in enumerate(pieces) if piece is array]
+                    if not known:
+                        pieces.append(array)
+                    piece = known[0] if known else len(pieces) - 1
+                    start = begin[letter] - begin[letters[0]]
+                    if copies and copies[-1][0] == piece and copies[-1][1] + copies[-1][3] == at:
+                        copies[-1] = copies[-1][:3] + (copies[-1][3] + size[letter],)
+                    else:
+                        copies.append((piece, at, start, size[letter]))
+                parts.append(tuple(copies))
+            rows = sum(size[letter] for letter in letters)
+            plan.append((begin[letters[0]], rows, slot, tuple(parts)))
         return tuple(plan), pieces
 
     up_keys, down_keys = [(1, 0, "b"), (1, 1, "b")], [(3, 3, "b"), (3, 2, "b")]
@@ -398,14 +412,14 @@
         integral_cols,
         live_slots,
         [four, other_four, far_four, far_other],
-        *planned(("p", 0, ORDER[:14]), ("q", 0, ORDER[:14]), ("b", 3, ORDER[3:15])),
+        *planned(("pq", 0, ORDER[:14]), ("b", 3, ORDER[3:15])),
     )
     last = [(2, 2), (0, 2)]
     return late_matmul(
         tail,
         total,
         (virtual_sum, pair_energy),
-        *planned(("p", 3, last), ("q", 3, last), ("b", 0, [(2, 0), (2, 1), (2, 3), (2, 2)])),
+        *planned(("pq", 3, last), ("b", 0, [(2, 0), (2, 1), (2, 3), (2, 2)])),
     )
 
 

time: 156 us -> 154 us (0.987)
  Pallas kernels: 42.5 us -> 40.8 us
where the time goes in v3:
time: 154 us; the launch traced here: 151 us
  waiting for transfers between devices  60.4 us (39%)
  Pallas kernels  40.8 us (26%)
  starting transfers between devices  37.5 us (24%)
  local copies, waits for them, and re-layouts  9.61 us (6%)
  matrix products  2.17 us (1%)
    ppermute x17, waiting for transfers between devices, virt_shift(): return lax.ppermute(array, 'virt', pairs)  56.3 us
    ppermute x17, starting transfers between devices, virt_shift(): return lax.ppermute(array, 'virt', pairs)  30.7 us
    pallas_call x1, Pallas kernels, early_matmul(): pl.pallas_call(functools.partial(early_kernel, plan, len(tiles), len(piec...  18.4 us
    pallas_call x7, Pallas kernels, pack(): pl.pallas_call(functools.partial(pack_kernel, plan, len(arrays)), in_spec...  16.6 us
    unnamed x54, local copies, waits for them, and re-layouts  8.6 us
    ppermute x4, waiting for transfers between devices, pair_swap(): return lax.ppermute(array, 'pair', [(i, i ^ bit) for i in range(16)])  4.07 us
    ppermute x4, starting transfers between devices, pair_swap(): return lax.ppermute(array, 'pair', [(i, i ^ bit) for i in range(16)])  3.6 us
    pallas_call x1, Pallas kernels, late_matmul(): pl.pallas_call(functools.partial(late_kernel, plan, len(pieces)), in_spec...  3.49 us
  transfers between devices with their start and end apart: 22, of which 9 were waited for; matrix products, arithmetic and copies ran while one was open for 2% of the time, Pallas kernels for 25%

profile of v3, /device:TPU:32, one launch (start us, length us, event | category | flops | bytes accessed | tf_op | source)
XLA Modules:
  0.0 151.2 jit_solution(4816455842638001815)
XLA Ops:
  1.8 2.4 %shard_map.100 = (bf16[1536,256]{1,0:T(8,128)(2,1)}, bf16[1216,256]{1,0:T(8,128)(2,1)}) custom-call(s32[2,12]{1,0:T(2,128)} %bitcast.42, bf16[1536,256]{1,0:T(8,128)(2,1)} %amplitudes.1), custom_call_target="tpu_custom_call" | custom-call | tf_op jit(solution)/shard_map/pallas_call | solution.py:91
  4.3 4.0 %collective-permute-done.refs_1_ = bf16[1,8,128,128]{3,2,1,0:T(8,128)(2,1)S(1)} collective-permute-done((bf16[1,8,128,128]{3,2,1,0:T(8,128)(2,1)}, bf16[1,8,128,128]{3,2,1,0:T(8,128)(2,1)S(1)}, u32[]{:S(2)}, u32[]{:S(2)}) %collective-permute-start) | collective-permute-done | bytes 262176 | tf_op jit(solution)/shard_map/ppermute | solution.py:64
  11.5 3.3 %collective-permute-start.1 = (bf16[1216,256]{1,0:T(8,128)(2,1)}, bf16[1216,256]{1,0:T(8,128)(2,1)S(1)}, u32[]{:S(2)}, u32[]{:S(2)}) collective-permute-start(bf16[1216,256]{1,0:T(8,128)(2,1)} %get-tuple-element.65), channel_id=1, source_target_pairs={{0,4},{1,5},{2,6},{3,7},{4,8},{5,9},{6,10},{7,11},{8,12},{9,13},{1... | collective-permute-start | bytes 1867784 | tf_op jit(solution)/shard_map/ppermute | solution.py:60
  14.8 2.1 %collective-permute-start.2 = (bf16[1216,256]{1,0:T(8,128)(2,1)}, bf16[1216,256]{1,0:T(8,128)(2,1)S(1)}, u32[]{:S(2)}, u32[]{:S(2)}) collective-permute-start(bf16[1216,256]{1,0:T(8,128)(2,1)} %get-tuple-element.65), channel_id=1, source_target_pairs={{0,12},{1,13},{2,14},{3,15},{4,0},{5,1},{6,2},{7,3},{8,4},{9,5},{1... | collective-permute-start | bytes 1867784 | tf_op jit(solution)/shard_map/ppermute | solution.py:60
  20.4 7.7 %collective-permute-done.4.refs_0_.refs_4_.refs_9_ = bf16[1536,256]{1,0:T(8,128)(2,1)S(1)} collective-permute-done((bf16[1536,256]{1,0:T(8,128)(2,1)}, bf16[1536,256]{1,0:T(8,128)(2,1)S(1)}, u32[]{:S(2)}, u32[]{:S(2)}) %collective-permute-start.4) | collective-permute-done | bytes 786464 | tf_op jit(solution)/shard_map/ppermute | solution.py:60
  31.8 2.2 %shard_map.103.refs_0_ = bf16[4,8,128,128]{3,2,1,0:T(8,128)(2,1)} custom-call(bf16[2,8,128,128]{3,2,1,0:T(8,128)(2,1)} %shard_map.102.refs_0_, bf16[2,8,128,128]{3,2,1,0:T(8,128)(2,1)} %copy-done.19), custom_call_target="tpu_custom_call" | custom-call | bytes 1048576 | tf_op jit(solution)/shard_map/pallas_call | solution.py:128
  34.0 9.0 %collective-permute-done.1.refs_0_.refs_11_ = bf16[1216,256]{1,0:T(8,128)(2,1)S(1)} collective-permute-done((bf16[1216,256]{1,0:T(8,128)(2,1)}, bf16[1216,256]{1,0:T(8,128)(2,1)S(1)}, u32[]{:S(2)}, u32[]{:S(2)}) %collective-permute-start.1) | collective-permute-done | bytes 622624 | tf_op jit(solution)/shard_map/ppermute | solution.py:60
  44.7 3.0 %shard_map.101 = (bf16[928,256]{1,0:T(8,128)(2,1)}, bf16[928,256]{1,0:T(8,128)(2,1)}, bf16[2432,256]{1,0:T(8,128)(2,1)}) custom-call(bf16[1216,256]{1,0:T(8,128)(2,1)} %copy-done.7, bf16[1536,256]{1,0:T(8,128)(2,1)} %get-tuple-element.66.refs_1_.refs_8_, bf16[1216,256]{1,0:T(8,128)(2,1)} %copy-done.9), custom_call_target="tpu_custom_call" | custom-call | bytes 2195456 | tf_op jit(solution)/shard_map/pallas_call | solution.py:128
  49.9 3.3 %collective-permute-start.11 = (bf16[4,8,128,128]{3,2,1,0:T(8,128)(2,1)}, bf16[4,8,128,128]{3,2,1,0:T(8,128)(2,1)}, u32[]{:S(2)}, u32[]{:S(2)}) collective-permute-start(bf16[4,8,128,128]{3,2,1,0:T(8,128)(2,1)} %shard_map.103.refs_0_), channel_id=1, source_target_pairs={{0,128},{16,144},{32,160},{48,176},{64,192},{80,208},{96,224},{112... | collective-permute-start | bytes 3145736 | tf_op jit(solution)/shard_map/ppermute | solution.py:68
  54.2 3.8 %collective-permute-start.7 = (bf16[928,256]{1,0:T(8,128)(2,1)S(1)}, bf16[928,256]{1,0:T(8,128)(2,1)S(1)}, u32[]{:S(2)}, u32[]{:S(2)}) collective-permute-start(bf16[928,256]{1,0:T(8,128)(2,1)S(1)} %copy-done.24), channel_id=1, source_target_pairs={{0,4},{1,5},{2,6},{3,7},{4,8},{5,9},{6,10},{7,11},{8,12},{9,13},{1... | collective-permute-start | bytes 1425416 | tf_op jit(solution)/shard_map/ppermute | solution.py:60
  59.7 1.9 %shard_map.105 = bf16[960,256]{1,0:T(8,128)(2,1)} custom-call(bf16[1536,256]{1,0:T(8,128)(2,1)} %copy-done, bf16[1536,256]{1,0:T(8,128)(2,1)} %copy-done.2, bf16[320,256]{1,0:T(8,128)(2,1)} %copy-done.15), custom_call_target="tpu_custom_call" | custom-call | bytes 491520 | tf_op jit(solution)/shard_map/pallas_call | solution.py:128
  61.6 9.7 %collective-permute-done.7.refs_0_.refs_4_ = bf16[928,256]{1,0:T(8,128)(2,1)S(1)} collective-permute-done((bf16[928,256]{1,0:T(8,128)(2,1)S(1)}, bf16[928,256]{1,0:T(8,128)(2,1)S(1)}, u32[]{:S(2)}, u32[]{:S(2)}) %collective-permute-start.7) | collective-permute-done | bytes 475168 | tf_op jit(solution)/shard_map/ppermute | solution.py:60
  71.3 5.9 %collective-permute-done.8.refs_1_.refs_5_ = bf16[928,256]{1,0:T(8,128)(2,1)S(1)} collective-permute-done((bf16[928,256]{1,0:T(8,128)(2,1)S(1)}, bf16[928,256]{1,0:T(8,128)(2,1)S(1)}, u32[]{:S(2)}, u32[]{:S(2)}) %collective-permute-start.8) | collective-permute-done | bytes 475168 | tf_op jit(solution)/shard_map/ppermute | solution.py:60
  77.3 2.1 %collective-permute-done.9.refs_2_.refs_13_ = bf16[2432,256]{1,0:T(8,128)(2,1)} collective-permute-done((bf16[2432,256]{1,0:T(8,128)(2,1)}, bf16[2432,256]{1,0:T(8,128)(2,1)}, u32[]{:S(2)}, u32[]{:S(2)}) %collective-permute-start.9) | collective-permute-done | bytes 1245216 | tf_op jit(solution)/shard_map/ppermute | solution.py:60
  79.4 3.1 %shard_map.106 = (bf16[2432,256]{1,0:T(8,128)(2,1)}, bf16[2432,256]{1,0:T(8,128)(2,1)}) custom-call(bf16[928,256]{1,0:T(8,128)(2,1)} %copy-done.4, bf16[928,256]{1,0:T(8,128)(2,1)} %copy-done.13, bf16[2432,256]{1,0:T(8,128)(2,1)} %collective-permute-done.9.refs_2_.refs_13_, bf16[2432,256]{1,0:T(8,128)(2,1)} %collective-permute-done.10.refs_3_.refs_14_), custom_call_target="tpu_custom_call" | custom-call | bytes 2490368 | tf_op jit(solution)/shard_map/pallas_call | solution.py:128
  82.7 3.2 %collective-permute-start.15 = (bf16[2432,256]{1,0:T(8,128)(2,1)}, bf16[2432,256]{1,0:T(8,128)(2,1)}, u32[]{:S(2)}, u32[]{:S(2)}) collective-permute-start(bf16[2432,256]{1,0:T(8,128)(2,1)} %get-tuple-element.81), channel_id=1, source_target_pairs={{0,3},{1,0},{2,1},{3,2},{4,7},{5,4},{6,5},{7,6},{8,11},{9,8},{10,9... | collective-permute-start | bytes 3735560 | tf_op jit(solution)/shard_map/ppermute | solution.py:60
  86.3 3.7 %collective-permute-start.13 = (bf16[960,256]{1,0:T(8,128)(2,1)}, bf16[960,256]{1,0:T(8,128)(2,1)}, u32[]{:S(2)}, u32[]{:S(2)}) collective-permute-start(bf16[960,256]{1,0:T(8,128)(2,1)} %shard_map.105), channel_id=1, source_target_pairs={{0,12},{1,13},{2,14},{3,15},{4,0},{5,1},{6,2},{7,3},{8,4},{9,5},{1... | collective-permute-start | bytes 1474568 | tf_op jit(solution)/shard_map/ppermute | solution.py:60
  90.1 16.4 %collective-permute-done.12.refs_1_.refs_15_ = bf16[960,256]{1,0:T(8,128)(2,1)S(1)} collective-permute-done((bf16[960,256]{1,0:T(8,128)(2,1)}, bf16[960,256]{1,0:T(8,128)(2,1)S(1)}, u32[]{:S(2)}, u32[]{:S(2)}) %collective-permute-start.12) | collective-permute-done | bytes 491552 | tf_op jit(solution)/shard_map/ppermute | solution.py:60
  106.4 5.5 %collective-permute-done.13.refs_2_.refs_16_ = bf16[960,256]{1,0:T(8,128)(2,1)} collective-permute-done((bf16[960,256]{1,0:T(8,128)(2,1)}, bf16[960,256]{1,0:T(8,128)(2,1)}, u32[]{:S(2)}, u32[]{:S(2)}) %collective-permute-start.13) | collective-permute-done | bytes 491552 | tf_op jit(solution)/shard_map/ppermute | solution.py:60
  111.9 2.9 %shard_map.107 = (bf16[640,256]{1,0:T(8,128)(2,1)}, bf16[640,256]{1,0:T(8,128)(2,1)}, bf16[1216,256]{1,0:T(8,128)(2,1)}, bf16[1216,256]{1,0:T(8,128)(2,1)}) custom-call(bf16[928,256]{1,0:T(8,128)(2,1)} %copy-done.4, bf16[960,256]{1,0:T(8,128)(2,1)} %copy-done.11, bf16[960,256]{1,0:T(8,128)(2,1)} %collective-permute-done.13.refs_2_.refs_16_, ...), custom_call_target="tpu_custom_call" | custom-call | bytes 1900544 | tf_op jit(solution)/shard_map/pallas_call | solution.py:128
  116.0 3.2 %collective-permute-start.19 = (bf16[1216,256]{1,0:T(8,128)(2,1)}, bf16[1216,256]{1,0:T(8,128)(2,1)S(1)}, u32[]{:S(2)}, u32[]{:S(2)}) collective-permute-start(bf16[1216,256]{1,0:T(8,128)(2,1)} %get-tuple-element.94), channel_id=1, source_target_pairs={{0,3},{1,0},{2,1},{3,2},{4,7},{5,4},{6,5},{7,6},{8,11},{9,8},{10,9... | collective-permute-start | bytes 1867784 | tf_op jit(solution)/shard_map/ppermute | solution.py:60
  119.3 3.7 %collective-permute-start.20 = (bf16[640,256]{1,0:T(8,128)(2,1)}, bf16[640,256]{1,0:T(8,128)(2,1)S(1)}, u32[]{:S(2)}, u32[]{:S(2)}) collective-permute-start(bf16[640,256]{1,0:T(8,128)(2,1)} %get-tuple-element.95), channel_id=1, source_target_pairs={{0,4},{1,5},{2,6},{3,7},{4,8},{5,9},{6,10},{7,11},{8,12},{9,13},{1... | collective-permute-start | bytes 983048 | tf_op jit(solution)/shard_map/ppermute | solution.py:60
  129.1 18.4 %shard_map.108 = (f32[1536,1024]{1,0:T(8,128)S(1)}, bf16[1280,1024]{1,0:T(8,128)(2,1)S(1)}) custom-call(s32[32]{0:T(128)S(1)} %dynamic-slice_bitcast_fusion.where, s32[8,16]{1,0:T(8,128)S(1)} %copy-done.17, s32[8]{0:T(128)S(1)} %copy-done.18, bf16[4,8,128,128]{3,2,1,0:T(8,128)(2,1)} %shard_map.103.refs_0_, ...), custom_call_target="tpu_custom_call" | custom-call | flops 10938744832 | bytes 27459584 | tf_op jit(solution)/shard_map/pallas_call | solution.py:253
  147.5 3.5 %shard_map.109 = bf16[1536,1024]{1,0:T(8,128)(2,1)} custom-call(bf16[1280,1024]{1,0:T(8,128)(2,1)S(1)} %get-tuple-element.89.weights, f32[1536,1024]{1,0:T(8,128)S(1)} %get-tuple-element.90.total, f32[1,1024]{1,0:T(1,128)S(1)} %bitcast.38, f32[1536,1]{1,0:T(8,128)S(1)} %copy.12.pair_energy, bf16[1216,256]{1,0:T(8,128)(2,1)S(1)} %collective-permute-done.18.refs_0_, ...), custom_call_target="tpu_custom_call" | custom-call | flops 1946157056 | bytes 14483456 | tf_op jit(solution)/shard_map/pallas_call | solution.py:274
  (94 shorter events, 26.5 us)
Async XLA Ops:
  0.0 8.3 %collective-permute-start = (bf16[1,8,128,128]{3,2,1,0:T(8,128)(2,1)}, bf16[1,8,128,128]{3,2,1,0:T(8,128)(2,1)S(1)}, u32[]{:S(2)}, u32[]{:S(2)}) collective-permute-start(bf16[1,8,128,128]{3,2,1,0:T(8,128)(2,1)} %bitcast.39), channel_id=1, source_target_pairs={{0,32},{16,48},{32,0},{48,16},{64,96},{80,112},{96,64},{112,80},{1... | collective-permute-start | bytes 786440 | tf_op jit(solution)/shard_map/ppermute | solution.py:64
  8.3 19.8 %collective-permute-start.4 = (bf16[1536,256]{1,0:T(8,128)(2,1)}, bf16[1536,256]{1,0:T(8,128)(2,1)S(1)}, u32[]{:S(2)}, u32[]{:S(2)}) collective-permute-start(bf16[1536,256]{1,0:T(8,128)(2,1)} %get-tuple-element.66.refs_1_.refs_8_), channel_id=1, source_target_pairs={{0,1},{1,2},{2,3},{3,0},{4,5},{5,6},{6,7},{7,4},{8,9},{9,10},{10,1... | collective-permute-start | bytes 2359304 | tf_op jit(solution)/shard_map/ppermute | solution.py:60
  9.8 38.0 %collective-permute-start.5 = (bf16[1536,256]{1,0:T(8,128)(2,1)}, bf16[1536,256]{1,0:T(8,128)(2,1)S(1)}, u32[]{:S(2)}, u32[]{:S(2)}) collective-permute-start(bf16[1536,256]{1,0:T(8,128)(2,1)} %get-tuple-element.66.refs_1_.refs_8_), channel_id=1, source_target_pairs={{0,3},{1,0},{2,1},{3,2},{4,7},{5,4},{6,5},{7,6},{8,11},{9,8},{10,9... | collective-permute-start | bytes 2359304 | tf_op jit(solution)/shard_map/ppermute | solution.py:60
  11.5 31.5 %collective-permute-start.1 = (bf16[1216,256]{1,0:T(8,128)(2,1)}, bf16[1216,256]{1,0:T(8,128)(2,1)S(1)}, u32[]{:S(2)}, u32[]{:S(2)}) collective-permute-start(bf16[1216,256]{1,0:T(8,128)(2,1)} %get-tuple-element.65), channel_id=1, source_target_pairs={{0,4},{1,5},{2,6},{3,7},{4,8},{5,9},{6,10},{7,11},{8,12},{9,13},{1... | collective-permute-start | bytes 1867784 | tf_op jit(solution)/shard_map/ppermute | solution.py:60
  14.8 28.3 %collective-permute-start.2 = (bf16[1216,256]{1,0:T(8,128)(2,1)}, bf16[1216,256]{1,0:T(8,128)(2,1)S(1)}, u32[]{:S(2)}, u32[]{:S(2)}) collective-permute-start(bf16[1216,256]{1,0:T(8,128)(2,1)} %get-tuple-element.65), channel_id=1, source_target_pairs={{0,12},{1,13},{2,14},{3,15},{4,0},{5,1},{6,2},{7,3},{8,4},{9,5},{1... | collective-permute-start | bytes 1867784 | tf_op jit(solution)/shard_map/ppermute | solution.py:60
  18.8 12.2 %collective-permute-start.3 = (bf16[2,8,128,128]{3,2,1,0:T(8,128)(2,1)}, bf16[2,8,128,128]{3,2,1,0:T(8,128)(2,1)S(1)}, u32[]{:S(2)}, u32[]{:S(2)}) collective-permute-start(bf16[2,8,128,128]{3,2,1,0:T(8,128)(2,1)} %shard_map.102.refs_0_), channel_id=1, source_target_pairs={{0,64},{16,80},{32,96},{48,112},{64,0},{80,16},{96,32},{112,48},{1... | collective-permute-start | bytes 1572872 | tf_op jit(solution)/shard_map/ppermute | solution.py:64
  30.6 17.2 %collective-permute-start.6 = (bf16[320,256]{1,0:T(8,128)(2,1)}, bf16[320,256]{1,0:T(8,128)(2,1)S(1)}, u32[]{:S(2)}, u32[]{:S(2)}) collective-permute-start(bf16[320,256]{1,0:T(8,128)(2,1)} %shard_map.104), channel_id=1, source_target_pairs={{0,1},{1,2},{2,3},{3,0},{4,5},{5,6},{6,7},{7,4},{8,9},{9,10},{10,1... | collective-permute-start | bytes 491528 | tf_op jit(solution)/shard_map/ppermute | solution.py:60
  47.8 29.5 %collective-permute-start.10 = (bf16[2432,256]{1,0:T(8,128)(2,1)}, bf16[2432,256]{1,0:T(8,128)(2,1)}, u32[]{:S(2)}, u32[]{:S(2)}) collective-permute-start(bf16[2432,256]{1,0:T(8,128)(2,1)} %get-tuple-element.73), channel_id=1, source_target_pairs={{0,3},{1,0},{2,1},{3,2},{4,7},{5,4},{6,5},{7,6},{8,11},{9,8},{10,9... | collective-permute-start | bytes 3735560 | tf_op jit(solution)/shard_map/ppermute | solution.py:60
  49.4 30.0 %collective-permute-start.9 = (bf16[2432,256]{1,0:T(8,128)(2,1)}, bf16[2432,256]{1,0:T(8,128)(2,1)}, u32[]{:S(2)}, u32[]{:S(2)}) collective-permute-start(bf16[2432,256]{1,0:T(8,128)(2,1)} %get-tuple-element.73), channel_id=1, source_target_pairs={{0,1},{1,2},{2,3},{3,0},{4,5},{5,6},{6,7},{7,4},{8,9},{9,10},{10,1... | collective-permute-start | bytes 3735560 | tf_op jit(solution)/shard_map/ppermute | solution.py:60
  49.9 32.6 %collective-permute-start.11 = (bf16[4,8,128,128]{3,2,1,0:T(8,128)(2,1)}, bf16[4,8,128,128]{3,2,1,0:T(8,128)(2,1)}, u32[]{:S(2)}, u32[]{:S(2)}) collective-permute-start(bf16[4,8,128,128]{3,2,1,0:T(8,128)(2,1)} %shard_map.103.refs_0_), channel_id=1, source_target_pairs={{0,128},{16,144},{32,160},{48,176},{64,192},{80,208},{96,224},{112... | collective-permute-start | bytes 3145736 | tf_op jit(solution)/shard_map/ppermute | solution.py:68
  54.2 17.1 %collective-permute-start.7 = (bf16[928,256]{1,0:T(8,128)(2,1)S(1)}, bf16[928,256]{1,0:T(8,128)(2,1)S(1)}, u32[]{:S(2)}, u32[]{:S(2)}) collective-permute-start(bf16[928,256]{1,0:T(8,128)(2,1)S(1)} %copy-done.24), channel_id=1, source_target_pairs={{0,4},{1,5},{2,6},{3,7},{4,8},{5,9},{6,10},{7,11},{8,12},{9,13},{1... | collective-permute-start | bytes 1425416 | tf_op jit(solution)/shard_map/ppermute | solution.py:60
  58.0 19.3 %collective-permute-start.8 = (bf16[928,256]{1,0:T(8,128)(2,1)S(1)}, bf16[928,256]{1,0:T(8,128)(2,1)S(1)}, u32[]{:S(2)}, u32[]{:S(2)}) collective-permute-start(bf16[928,256]{1,0:T(8,128)(2,1)S(1)} %copy-done.23), channel_id=1, source_target_pairs={{0,12},{1,13},{2,14},{3,15},{4,0},{5,1},{6,2},{7,3},{8,4},{9,5},{1... | collective-permute-start | bytes 1425416 | tf_op jit(solution)/shard_map/ppermute | solution.py:60
  82.5 41.3 %copy-start.1 = (bf16[1536,256]{1,0:T(8,128)(2,1)S(1)}, bf16[1536,256]{1,0:T(8,128)(2,1)}, u32[]{:S(2)}) copy-start(bf16[1536,256]{1,0:T(8,128)(2,1)} %copy-done) | copy-start | bytes 2359300
  82.6 41.3 %copy-start.3 = (bf16[1536,256]{1,0:T(8,128)(2,1)S(1)}, bf16[1536,256]{1,0:T(8,128)(2,1)}, u32[]{:S(2)}) copy-start(bf16[1536,256]{1,0:T(8,128)(2,1)} %copy-done.2) | copy-start | bytes 2359300
  82.6 29.3 %collective-permute-start.14 = (bf16[2432,256]{1,0:T(8,128)(2,1)}, bf16[2432,256]{1,0:T(8,128)(2,1)}, u32[]{:S(2)}, u32[]{:S(2)}) collective-permute-start(bf16[2432,256]{1,0:T(8,128)(2,1)} %get-tuple-element.80), channel_id=1, source_target_pairs={{0,1},{1,2},{2,3},{3,0},{4,5},{5,6},{6,7},{7,4},{8,9},{9,10},{10,1... | collective-permute-start | bytes 3735560 | tf_op jit(solution)/shard_map/ppermute | solution.py:60
  82.7 29.2 %collective-permute-start.15 = (bf16[2432,256]{1,0:T(8,128)(2,1)}, bf16[2432,256]{1,0:T(8,128)(2,1)}, u32[]{:S(2)}, u32[]{:S(2)}) collective-permute-start(bf16[2432,256]{1,0:T(8,128)(2,1)} %get-tuple-element.81), channel_id=1, source_target_pairs={{0,3},{1,0},{2,1},{3,2},{4,7},{5,4},{6,5},{7,6},{8,11},{9,8},{10,9... | collective-permute-start | bytes 3735560 | tf_op jit(solution)/shard_map/ppermute | solution.py:60
  85.9 28.9 %collective-permute-start.16 = (bf16[4,8,128,128]{3,2,1,0:T(8,128)(2,1)}, bf16[4,8,128,128]{3,2,1,0:T(8,128)(2,1)}, u32[]{:S(2)}, u32[]{:S(2)}) collective-permute-start(bf16[4,8,128,128]{3,2,1,0:T(8,128)(2,1)} %collective-permute-done.11.refs_2_), channel_id=1, source_target_pairs={{0,16},{16,0},{32,48},{48,32},{64,80},{80,64},{96,112},{112,96},{1... | collective-permute-start | bytes 3145736 | tf_op jit(solution)/shard_map/ppermute | solution.py:64
  85.9 20.5 %collective-permute-start.12 = (bf16[960,256]{1,0:T(8,128)(2,1)}, bf16[960,256]{1,0:T(8,128)(2,1)S(1)}, u32[]{:S(2)}, u32[]{:S(2)}) collective-permute-start(bf16[960,256]{1,0:T(8,128)(2,1)} %shard_map.105), channel_id=1, source_target_pairs={{0,4},{1,5},{2,6},{3,7},{4,8},{5,9},{6,10},{7,11},{8,12},{9,13},{1... | collective-permute-start | bytes 1474568 | tf_op jit(solution)/shard_map/ppermute | solution.py:60
  86.3 25.5 %collective-permute-start.13 = (bf16[960,256]{1,0:T(8,128)(2,1)}, bf16[960,256]{1,0:T(8,128)(2,1)}, u32[]{:S(2)}, u32[]{:S(2)}) collective-permute-start(bf16[960,256]{1,0:T(8,128)(2,1)} %shard_map.105), channel_id=1, source_target_pairs={{0,12},{1,13},{2,14},{3,15},{4,0},{5,1},{6,2},{7,3},{8,4},{9,5},{1... | collective-permute-start | bytes 1474568 | tf_op jit(solution)/shard_map/ppermute | solution.py:60
  114.8 9.0 %collective-permute-start.17 = (bf16[4,8,128,128]{3,2,1,0:T(8,128)(2,1)}, bf16[4,8,128,128]{3,2,1,0:T(8,128)(2,1)}, u32[]{:S(2)}, u32[]{:S(2)}) collective-permute-start(bf16[4,8,128,128]{3,2,1,0:T(8,128)(2,1)} %shard_map.103.refs_0_), channel_id=1, source_target_pairs={{0,16},{16,0},{32,48},{48,32},{64,80},{80,64},{96,112},{112,96},{1... | collective-permute-start | bytes 3145736 | tf_op jit(solution)/shard_map/ppermute | solution.py:64
  115.9 31.5 %collective-permute-start.18 = (bf16[1216,256]{1,0:T(8,128)(2,1)}, bf16[1216,256]{1,0:T(8,128)(2,1)S(1)}, u32[]{:S(2)}, u32[]{:S(2)}) collective-permute-start(bf16[1216,256]{1,0:T(8,128)(2,1)} %get-tuple-element.93), channel_id=1, source_target_pairs={{0,1},{1,2},{2,3},{3,0},{4,5},{5,6},{6,7},{7,4},{8,9},{9,10},{10,1... | collective-permute-start | bytes 1867784 | tf_op jit(solution)/shard_map/ppermute | solution.py:60
  116.0 31.5 %collective-permute-start.19 = (bf16[1216,256]{1,0:T(8,128)(2,1)}, bf16[1216,256]{1,0:T(8,128)(2,1)S(1)}, u32[]{:S(2)}, u32[]{:S(2)}) collective-permute-start(bf16[1216,256]{1,0:T(8,128)(2,1)} %get-tuple-element.94), channel_id=1, source_target_pairs={{0,3},{1,0},{2,1},{3,2},{4,7},{5,4},{6,5},{7,6},{8,11},{9,8},{10,9... | collective-permute-start | bytes 1867784 | tf_op jit(solution)/shard_map/ppermute | solution.py:60
  119.3 28.2 %collective-permute-start.20 = (bf16[640,256]{1,0:T(8,128)(2,1)}, bf16[640,256]{1,0:T(8,128)(2,1)S(1)}, u32[]{:S(2)}, u32[]{:S(2)}) collective-permute-start(bf16[640,256]{1,0:T(8,128)(2,1)} %get-tuple-element.95), channel_id=1, source_target_pairs={{0,4},{1,5},{2,6},{3,7},{4,8},{5,9},{6,10},{7,11},{8,12},{9,13},{1... | collective-permute-start | bytes 983048 | tf_op jit(solution)/shard_map/ppermute | solution.py:60
  123.0 24.5 %collective-permute-start.21 = (bf16[640,256]{1,0:T(8,128)(2,1)}, bf16[640,256]{1,0:T(8,128)(2,1)S(1)}, u32[]{:S(2)}, u32[]{:S(2)}) collective-permute-start(bf16[640,256]{1,0:T(8,128)(2,1)} %get-tuple-element.96), channel_id=1, source_target_pairs={{0,12},{1,13},{2,14},{3,15},{4,0},{5,1},{6,2},{7,3},{8,4},{9,5},{1... | collective-permute-start | bytes 983048 | tf_op jit(solution)/shard_map/ppermute | solution.py:60
  (25 other events, 321.7 us)

commit v4 on v3

--- a/solution.py
+++ b/solution.py
@@ -15,7 +15,7 @@
 LATE_VMEM = 16 * 1024 * 1024
 RING = 4
 CROSS_ROWS = 320
-GROUP = 5
+GROUP = 7
 ORDER = (
     [(2, 0), (2, 1), (2, 3)]
     + [(0, 0), (0, 1), (0, 3), (1, 0), (3, 0), (1, 1), (1, 3), (3, 1), (3, 3), (1, 2), (3, 2)]

time: 154 us -> 154 us (level)
  transfers between devices with their start and end apart: 22 -> 22, of which waited for: 9 -> 9; matrix products, arithmetic and copies ran while one was open for 2% -> 2% of each run, Pallas kernels for 25% -> 24%
where the time goes in v4:
time: 154 us; the launch traced here: 151 us
  waiting for transfers between devices  60.4 us (39%)
  Pallas kernels  40.4 us (26%)
  starting transfers between devices  37.5 us (24%)
  local copies, waits for them, and re-layouts  9.61 us (6%)
  matrix products  2.17 us (1%)
    ppermute x17, waiting for transfers between devices, virt_shift(): return lax.ppermute(array, 'virt', pairs)  56.3 us
    ppermute x17, starting transfers between devices, virt_shift(): return lax.ppermute(array, 'virt', pairs)  30.7 us
    pallas_call x1, Pallas kernels, early_matmul(): pl.pallas_call(functools.partial(early_kernel, plan, len(tiles), len(piec...  17.9 us
    pallas_call x7, Pallas kernels, pack(): pl.pallas_call(functools.partial(pack_kernel, plan, len(arrays)), in_spec...  16.6 us
    unnamed x54, local copies, waits for them, and re-layouts  8.6 us
    ppermute x4, waiting for transfers between devices, pair_swap(): return lax.ppermute(array, 'pair', [(i, i ^ bit) for i in range(16)])  4.07 us
    ppermute x4, starting transfers between devices, pair_swap(): return lax.ppermute(array, 'pair', [(i, i ^ bit) for i in range(16)])  3.6 us
    pallas_call x1, Pallas kernels, late_matmul(): pl.pallas_call(functools.partial(late_kernel, plan, len(pieces)), in_spec...  3.49 us
  transfers between devices with their start and end apart: 22, of which 9 were waited for; matrix products, arithmetic and copies ran while one was open for 2% of the time, Pallas kernels for 24%

profile of v4, /device:TPU:32, one launch (start us, length us, event | category | flops | bytes accessed | tf_op | source)
XLA Modules:
  0.0 150.7 jit_solution(17595176103339647427)
XLA Ops:
  1.8 2.4 %shard_map.100 = (bf16[1536,256]{1,0:T(8,128)(2,1)}, bf16[1216,256]{1,0:T(8,128)(2,1)}) custom-call(s32[2,12]{1,0:T(2,128)} %bitcast.42, bf16[1536,256]{1,0:T(8,128)(2,1)} %amplitudes.1), custom_call_target="tpu_custom_call" | custom-call | tf_op jit(solution)/shard_map/pallas_call | solution.py:91
  4.3 4.0 %collective-permute-done.refs_1_ = bf16[1,8,128,128]{3,2,1,0:T(8,128)(2,1)S(1)} collective-permute-done((bf16[1,8,128,128]{3,2,1,0:T(8,128)(2,1)}, bf16[1,8,128,128]{3,2,1,0:T(8,128)(2,1)S(1)}, u32[]{:S(2)}, u32[]{:S(2)}) %collective-permute-start) | collective-permute-done | bytes 262176 | tf_op jit(solution)/shard_map/ppermute | solution.py:64
  11.5 3.3 %collective-permute-start.1 = (bf16[1216,256]{1,0:T(8,128)(2,1)}, bf16[1216,256]{1,0:T(8,128)(2,1)S(1)}, u32[]{:S(2)}, u32[]{:S(2)}) collective-permute-start(bf16[1216,256]{1,0:T(8,128)(2,1)} %get-tuple-element.65), channel_id=1, source_target_pairs={{0,4},{1,5},{2,6},{3,7},{4,8},{5,9},{6,10},{7,11},{8,12},{9,13},{1... | collective-permute-start | bytes 1867784 | tf_op jit(solution)/shard_map/ppermute | solution.py:60
  14.8 2.1 %collective-permute-start.2 = (bf16[1216,256]{1,0:T(8,128)(2,1)}, bf16[1216,256]{1,0:T(8,128)(2,1)S(1)}, u32[]{:S(2)}, u32[]{:S(2)}) collective-permute-start(bf16[1216,256]{1,0:T(8,128)(2,1)} %get-tuple-element.65), channel_id=1, source_target_pairs={{0,12},{1,13},{2,14},{3,15},{4,0},{5,1},{6,2},{7,3},{8,4},{9,5},{1... | collective-permute-start | bytes 1867784 | tf_op jit(solution)/shard_map/ppermute | solution.py:60
  20.4 7.7 %collective-permute-done.4.refs_0_.refs_4_.refs_9_ = bf16[1536,256]{1,0:T(8,128)(2,1)S(1)} collective-permute-done((bf16[1536,256]{1,0:T(8,128)(2,1)}, bf16[1536,256]{1,0:T(8,128)(2,1)S(1)}, u32[]{:S(2)}, u32[]{:S(2)}) %collective-permute-start.4) | collective-permute-done | bytes 786464 | tf_op jit(solution)/shard_map/ppermute | solution.py:60
  31.8 2.2 %shard_map.103.refs_0_ = bf16[4,8,128,128]{3,2,1,0:T(8,128)(2,1)} custom-call(bf16[2,8,128,128]{3,2,1,0:T(8,128)(2,1)} %shard_map.102.refs_0_, bf16[2,8,128,128]{3,2,1,0:T(8,128)(2,1)} %copy-done.19), custom_call_target="tpu_custom_call" | custom-call | bytes 1048576 | tf_op jit(solution)/shard_map/pallas_call | solution.py:128
  34.0 9.0 %collective-permute-done.1.refs_0_.refs_11_ = bf16[1216,256]{1,0:T(8,128)(2,1)S(1)} collective-permute-done((bf16[1216,256]{1,0:T(8,128)(2,1)}, bf16[1216,256]{1,0:T(8,128)(2,1)S(1)}, u32[]{:S(2)}, u32[]{:S(2)}) %collective-permute-start.1) | collective-permute-done | bytes 622624 | tf_op jit(solution)/shard_map/ppermute | solution.py:60
  44.7 3.0 %shard_map.101 = (bf16[928,256]{1,0:T(8,128)(2,1)}, bf16[928,256]{1,0:T(8,128)(2,1)}, bf16[2432,256]{1,0:T(8,128)(2,1)}) custom-call(bf16[1216,256]{1,0:T(8,128)(2,1)} %copy-done.7, bf16[1536,256]{1,0:T(8,128)(2,1)} %get-tuple-element.66.refs_1_.refs_8_, bf16[1216,256]{1,0:T(8,128)(2,1)} %copy-done.9), custom_call_target="tpu_custom_call" | custom-call | bytes 2195456 | tf_op jit(solution)/shard_map/pallas_call | solution.py:128
  49.9 3.3 %collective-permute-start.11 = (bf16[4,8,128,128]{3,2,1,0:T(8,128)(2,1)}, bf16[4,8,128,128]{3,2,1,0:T(8,128)(2,1)}, u32[]{:S(2)}, u32[]{:S(2)}) collective-permute-start(bf16[4,8,128,128]{3,2,1,0:T(8,128)(2,1)} %shard_map.103.refs_0_), channel_id=1, source_target_pairs={{0,128},{16,144},{32,160},{48,176},{64,192},{80,208},{96,224},{112... | collective-permute-start | bytes 3145736 | tf_op jit(solution)/shard_map/ppermute | solution.py:68
  54.2 3.8 %collective-permute-start.7 = (bf16[928,256]{1,0:T(8,128)(2,1)S(1)}, bf16[928,256]{1,0:T(8,128)(2,1)S(1)}, u32[]{:S(2)}, u32[]{:S(2)}) collective-permute-start(bf16[928,256]{1,0:T(8,128)(2,1)S(1)} %copy-done.24), channel_id=1, source_target_pairs={{0,4},{1,5},{2,6},{3,7},{4,8},{5,9},{6,10},{7,11},{8,12},{9,13},{1... | collective-permute-start | bytes 1425416 | tf_op jit(solution)/shard_map/ppermute | solution.py:60
  59.7 1.9 %shard_map.105 = bf16[960,256]{1,0:T(8,128)(2,1)} custom-call(bf16[1536,256]{1,0:T(8,128)(2,1)} %copy-done, bf16[1536,256]{1,0:T(8,128)(2,1)} %copy-done.2, bf16[320,256]{1,0:T(8,128)(2,1)} %copy-done.15), custom_call_target="tpu_custom_call" | custom-call | bytes 491520 | tf_op jit(solution)/shard_map/pallas_call | solution.py:128
  61.6 9.7 %collective-permute-done.7.refs_0_.refs_4_ = bf16[928,256]{1,0:T(8,128)(2,1)S(1)} collective-permute-done((bf16[928,256]{1,0:T(8,128)(2,1)S(1)}, bf16[928,256]{1,0:T(8,128)(2,1)S(1)}, u32[]{:S(2)}, u32[]{:S(2)}) %collective-permute-start.7) | collective-permute-done | bytes 475168 | tf_op jit(solution)/shard_map/ppermute | solution.py:60
  71.3 5.9 %collective-permute-done.8.refs_1_.refs_5_ = bf16[928,256]{1,0:T(8,128)(2,1)S(1)} collective-permute-done((bf16[928,256]{1,0:T(8,128)(2,1)S(1)}, bf16[928,256]{1,0:T(8,128)(2,1)S(1)}, u32[]{:S(2)}, u32[]{:S(2)}) %collective-permute-start.8) | collective-permute-done | bytes 475168 | tf_op jit(solution)/shard_map/ppermute | solution.py:60
  77.3 2.1 %collective-permute-done.9.refs_2_.refs_13_ = bf16[2432,256]{1,0:T(8,128)(2,1)} collective-permute-done((bf16[2432,256]{1,0:T(8,128)(2,1)}, bf16[2432,256]{1,0:T(8,128)(2,1)}, u32[]{:S(2)}, u32[]{:S(2)}) %collective-permute-start.9) | collective-permute-done | bytes 1245216 | tf_op jit(solution)/shard_map/ppermute | solution.py:60
  79.4 3.1 %shard_map.106 = (bf16[2432,256]{1,0:T(8,128)(2,1)}, bf16[2432,256]{1,0:T(8,128)(2,1)}) custom-call(bf16[928,256]{1,0:T(8,128)(2,1)} %copy-done.4, bf16[928,256]{1,0:T(8,128)(2,1)} %copy-done.13, bf16[2432,256]{1,0:T(8,128)(2,1)} %collective-permute-done.9.refs_2_.refs_13_, bf16[2432,256]{1,0:T(8,128)(2,1)} %collective-permute-done.10.refs_3_.refs_14_), custom_call_target="tpu_custom_call" | custom-call | bytes 2490368 | tf_op jit(solution)/shard_map/pallas_call | solution.py:128
  82.7 3.2 %collective-permute-start.15 = (bf16[2432,256]{1,0:T(8,128)(2,1)}, bf16[2432,256]{1,0:T(8,128)(2,1)}, u32[]{:S(2)}, u32[]{:S(2)}) collective-permute-start(bf16[2432,256]{1,0:T(8,128)(2,1)} %get-tuple-element.81), channel_id=1, source_target_pairs={{0,3},{1,0},{2,1},{3,2},{4,7},{5,4},{6,5},{7,6},{8,11},{9,8},{10,9... | collective-permute-start | bytes 3735560 | tf_op jit(solution)/shard_map/ppermute | solution.py:60
  86.3 3.7 %collective-permute-start.13 = (bf16[960,256]{1,0:T(8,128)(2,1)}, bf16[960,256]{1,0:T(8,128)(2,1)}, u32[]{:S(2)}, u32[]{:S(2)}) collective-permute-start(bf16[960,256]{1,0:T(8,128)(2,1)} %shard_map.105), channel_id=1, source_target_pairs={{0,12},{1,13},{2,14},{3,15},{4,0},{5,1},{6,2},{7,3},{8,4},{9,5},{1... | collective-permute-start | bytes 1474568 | tf_op jit(solution)/shard_map/ppermute | solution.py:60
  90.1 16.4 %collective-permute-done.12.refs_1_.refs_15_ = bf16[960,256]{1,0:T(8,128)(2,1)S(1)} collective-permute-done((bf16[960,256]{1,0:T(8,128)(2,1)}, bf16[960,256]{1,0:T(8,128)(2,1)S(1)}, u32[]{:S(2)}, u32[]{:S(2)}) %collective-permute-start.12) | collective-permute-done | bytes 491552 | tf_op jit(solution)/shard_map/ppermute | solution.py:60
  106.4 5.5 %collective-permute-done.13.refs_2_.refs_16_ = bf16[960,256]{1,0:T(8,128)(2,1)} collective-permute-done((bf16[960,256]{1,0:T(8,128)(2,1)}, bf16[960,256]{1,0:T(8,128)(2,1)}, u32[]{:S(2)}, u32[]{:S(2)}) %collective-permute-start.13) | collective-permute-done | bytes 491552 | tf_op jit(solution)/shard_map/ppermute | solution.py:60
  111.9 2.9 %shard_map.107 = (bf16[640,256]{1,0:T(8,128)(2,1)}, bf16[640,256]{1,0:T(8,128)(2,1)}, bf16[1216,256]{1,0:T(8,128)(2,1)}, bf16[1216,256]{1,0:T(8,128)(2,1)}) custom-call(bf16[928,256]{1,0:T(8,128)(2,1)} %copy-done.4, bf16[960,256]{1,0:T(8,128)(2,1)} %copy-done.11, bf16[960,256]{1,0:T(8,128)(2,1)} %collective-permute-done.13.refs_2_.refs_16_, ...), custom_call_target="tpu_custom_call" | custom-call | bytes 1900544 | tf_op jit(solution)/shard_map/pallas_call | solution.py:128
  116.0 3.2 %collective-permute-start.19 = (bf16[1216,256]{1,0:T(8,128)(2,1)}, bf16[1216,256]{1,0:T(8,128)(2,1)S(1)}, u32[]{:S(2)}, u32[]{:S(2)}) collective-permute-start(bf16[1216,256]{1,0:T(8,128)(2,1)} %get-tuple-element.94), channel_id=1, source_target_pairs={{0,3},{1,0},{2,1},{3,2},{4,7},{5,4},{6,5},{7,6},{8,11},{9,8},{10,9... | collective-permute-start | bytes 1867784 | tf_op jit(solution)/shard_map/ppermute | solution.py:60
  119.3 3.7 %collective-permute-start.20 = (bf16[640,256]{1,0:T(8,128)(2,1)}, bf16[640,256]{1,0:T(8,128)(2,1)S(1)}, u32[]{:S(2)}, u32[]{:S(2)}) collective-permute-start(bf16[640,256]{1,0:T(8,128)(2,1)} %get-tuple-element.95), channel_id=1, source_target_pairs={{0,4},{1,5},{2,6},{3,7},{4,8},{5,9},{6,10},{7,11},{8,12},{9,13},{1... | collective-permute-start | bytes 983048 | tf_op jit(solution)/shard_map/ppermute | solution.py:60
  129.1 17.9 %shard_map.108 = (f32[1536,1024]{1,0:T(8,128)S(1)}, bf16[1280,1024]{1,0:T(8,128)(2,1)S(1)}) custom-call(s32[32]{0:T(128)S(1)} %dynamic-slice_bitcast_fusion.where, s32[8,16]{1,0:T(8,128)S(1)} %copy-done.17, s32[8]{0:T(128)S(1)} %copy-done.18, bf16[4,8,128,128]{3,2,1,0:T(8,128)(2,1)} %shard_map.103.refs_0_, ...), custom_call_target="tpu_custom_call" | custom-call | flops 10938744832 | bytes 27459584 | tf_op jit(solution)/shard_map/pallas_call | solution.py:253
  147.1 3.5 %shard_map.109 = bf16[1536,1024]{1,0:T(8,128)(2,1)} custom-call(bf16[1280,1024]{1,0:T(8,128)(2,1)S(1)} %get-tuple-element.89.weights, f32[1536,1024]{1,0:T(8,128)S(1)} %get-tuple-element.90.total, f32[1,1024]{1,0:T(1,128)S(1)} %bitcast.38, f32[1536,1]{1,0:T(8,128)S(1)} %copy.12.pair_energy, bf16[1216,256]{1,0:T(8,128)(2,1)S(1)} %collective-permute-done.18.refs_0_, ...), custom_call_target="tpu_custom_call" | custom-call | flops 1946157056 | bytes 14483456 | tf_op jit(solution)/shard_map/pallas_call | solution.py:274
  (94 shorter events, 26.5 us)
Async XLA Ops:
  0.0 8.3 %collective-permute-start = (bf16[1,8,128,128]{3,2,1,0:T(8,128)(2,1)}, bf16[1,8,128,128]{3,2,1,0:T(8,128)(2,1)S(1)}, u32[]{:S(2)}, u32[]{:S(2)}) collective-permute-start(bf16[1,8,128,128]{3,2,1,0:T(8,128)(2,1)} %bitcast.39), channel_id=1, source_target_pairs={{0,32},{16,48},{32,0},{48,16},{64,96},{80,112},{96,64},{112,80},{1... | collective-permute-start | bytes 786440 | tf_op jit(solution)/shard_map/ppermute | solution.py:64
  8.3 19.8 %collective-permute-start.4 = (bf16[1536,256]{1,0:T(8,128)(2,1)}, bf16[1536,256]{1,0:T(8,128)(2,1)S(1)}, u32[]{:S(2)}, u32[]{:S(2)}) collective-permute-start(bf16[1536,256]{1,0:T(8,128)(2,1)} %get-tuple-element.66.refs_1_.refs_8_), channel_id=1, source_target_pairs={{0,1},{1,2},{2,3},{3,0},{4,5},{5,6},{6,7},{7,4},{8,9},{9,10},{10,1... | collective-permute-start | bytes 2359304 | tf_op jit(solution)/shard_map/ppermute | solution.py:60
  9.8 38.0 %collective-permute-start.5 = (bf16[1536,256]{1,0:T(8,128)(2,1)}, bf16[1536,256]{1,0:T(8,128)(2,1)S(1)}, u32[]{:S(2)}, u32[]{:S(2)}) collective-permute-start(bf16[1536,256]{1,0:T(8,128)(2,1)} %get-tuple-element.66.refs_1_.refs_8_), channel_id=1, source_target_pairs={{0,3},{1,0},{2,1},{3,2},{4,7},{5,4},{6,5},{7,6},{8,11},{9,8},{10,9... | collective-permute-start | bytes 2359304 | tf_op jit(solution)/shard_map/ppermute | solution.py:60
  11.5 31.5 %collective-permute-start.1 = (bf16[1216,256]{1,0:T(8,128)(2,1)}, bf16[1216,256]{1,0:T(8,128)(2,1)S(1)}, u32[]{:S(2)}, u32[]{:S(2)}) collective-permute-start(bf16[1216,256]{1,0:T(8,128)(2,1)} %get-tuple-element.65), channel_id=1, source_target_pairs={{0,4},{1,5},{2,6},{3,7},{4,8},{5,9},{6,10},{7,11},{8,12},{9,13},{1... | collective-permute-start | bytes 1867784 | tf_op jit(solution)/shard_map/ppermute | solution.py:60
  14.8 28.3 %collective-permute-start.2 = (bf16[1216,256]{1,0:T(8,128)(2,1)}, bf16[1216,256]{1,0:T(8,128)(2,1)S(1)}, u32[]{:S(2)}, u32[]{:S(2)}) collective-permute-start(bf16[1216,256]{1,0:T(8,128)(2,1)} %get-tuple-element.65), channel_id=1, source_target_pairs={{0,12},{1,13},{2,14},{3,15},{4,0},{5,1},{6,2},{7,3},{8,4},{9,5},{1... | collective-permute-start | bytes 1867784 | tf_op jit(solution)/shard_map/ppermute | solution.py:60
  18.8 12.2 %collective-permute-start.3 = (bf16[2,8,128,128]{3,2,1,0:T(8,128)(2,1)}, bf16[2,8,128,128]{3,2,1,0:T(8,128)(2,1)S(1)}, u32[]{:S(2)}, u32[]{:S(2)}) collective-permute-start(bf16[2,8,128,128]{3,2,1,0:T(8,128)(2,1)} %shard_map.102.refs_0_), channel_id=1, source_target_pairs={{0,64},{16,80},{32,96},{48,112},{64,0},{80,16},{96,32},{112,48},{1... | collective-permute-start | bytes 1572872 | tf_op jit(solution)/shard_map/ppermute | solution.py:64
  30.6 17.2 %collective-permute-start.6 = (bf16[320,256]{1,0:T(8,128)(2,1)}, bf16[320,256]{1,0:T(8,128)(2,1)S(1)}, u32[]{:S(2)}, u32[]{:S(2)}) collective-permute-start(bf16[320,256]{1,0:T(8,128)(2,1)} %shard_map.104), channel_id=1, source_target_pairs={{0,1},{1,2},{2,3},{3,0},{4,5},{5,6},{6,7},{7,4},{8,9},{9,10},{10,1... | collective-permute-start | bytes 491528 | tf_op jit(solution)/shard_map/ppermute | solution.py:60
  47.8 29.5 %collective-permute-start.10 = (bf16[2432,256]{1,0:T(8,128)(2,1)}, bf16[2432,256]{1,0:T(8,128)(2,1)}, u32[]{:S(2)}, u32[]{:S(2)}) collective-permute-start(bf16[2432,256]{1,0:T(8,128)(2,1)} %get-tuple-element.73), channel_id=1, source_target_pairs={{0,3},{1,0},{2,1},{3,2},{4,7},{5,4},{6,5},{7,6},{8,11},{9,8},{10,9... | collective-permute-start | bytes 3735560 | tf_op jit(solution)/shard_map/ppermute | solution.py:60
  49.4 30.0 %collective-permute-start.9 = (bf16[2432,256]{1,0:T(8,128)(2,1)}, bf16[2432,256]{1,0:T(8,128)(2,1)}, u32[]{:S(2)}, u32[]{:S(2)}) collective-permute-start(bf16[2432,256]{1,0:T(8,128)(2,1)} %get-tuple-element.73), channel_id=1, source_target_pairs={{0,1},{1,2},{2,3},{3,0},{4,5},{5,6},{6,7},{7,4},{8,9},{9,10},{10,1... | collective-permute-start | bytes 3735560 | tf_op jit(solution)/shard_map/ppermute | solution.py:60
  49.9 32.6 %collective-permute-start.11 = (bf16[4,8,128,128]{3,2,1,0:T(8,128)(2,1)}, bf16[4,8,128,128]{3,2,1,0:T(8,128)(2,1)}, u32[]{:S(2)}, u32[]{:S(2)}) collective-permute-start(bf16[4,8,128,128]{3,2,1,0:T(8,128)(2,1)} %shard_map.103.refs_0_), channel_id=1, source_target_pairs={{0,128},{16,144},{32,160},{48,176},{64,192},{80,208},{96,224},{112... | collective-permute-start | bytes 3145736 | tf_op jit(solution)/shard_map/ppermute | solution.py:68
  54.2 17.1 %collective-permute-start.7 = (bf16[928,256]{1,0:T(8,128)(2,1)S(1)}, bf16[928,256]{1,0:T(8,128)(2,1)S(1)}, u32[]{:S(2)}, u32[]{:S(2)}) collective-permute-start(bf16[928,256]{1,0:T(8,128)(2,1)S(1)} %copy-done.24), channel_id=1, source_target_pairs={{0,4},{1,5},{2,6},{3,7},{4,8},{5,9},{6,10},{7,11},{8,12},{9,13},{1... | collective-permute-start | bytes 1425416 | tf_op jit(solution)/shard_map/ppermute | solution.py:60
  58.0 19.3 %collective-permute-start.8 = (bf16[928,256]{1,0:T(8,128)(2,1)S(1)}, bf16[928,256]{1,0:T(8,128)(2,1)S(1)}, u32[]{:S(2)}, u32[]{:S(2)}) collective-permute-start(bf16[928,256]{1,0:T(8,128)(2,1)S(1)} %copy-done.23), channel_id=1, source_target_pairs={{0,12},{1,13},{2,14},{3,15},{4,0},{5,1},{6,2},{7,3},{8,4},{9,5},{1... | collective-permute-start | bytes 1425416 | tf_op jit(solution)/shard_map/ppermute | solution.py:60
  82.5 41.3 %copy-start.1 = (bf16[1536,256]{1,0:T(8,128)(2,1)S(1)}, bf16[1536,256]{1,0:T(8,128)(2,1)}, u32[]{:S(2)}) copy-start(bf16[1536,256]{1,0:T(8,128)(2,1)} %copy-done) | copy-start | bytes 2359300
  82.6 41.3 %copy-start.3 = (bf16[1536,256]{1,0:T(8,128)(2,1)S(1)}, bf16[1536,256]{1,0:T(8,128)(2,1)}, u32[]{:S(2)}) copy-start(bf16[1536,256]{1,0:T(8,128)(2,1)} %copy-done.2) | copy-start | bytes 2359300
  82.6 29.3 %collective-permute-start.14 = (bf16[2432,256]{1,0:T(8,128)(2,1)}, bf16[2432,256]{1,0:T(8,128)(2,1)}, u32[]{:S(2)}, u32[]{:S(2)}) collective-permute-start(bf16[2432,256]{1,0:T(8,128)(2,1)} %get-tuple-element.80), channel_id=1, source_target_pairs={{0,1},{1,2},{2,3},{3,0},{4,5},{5,6},{6,7},{7,4},{8,9},{9,10},{10,1... | collective-permute-start | bytes 3735560 | tf_op jit(solution)/shard_map/ppermute | solution.py:60
  82.7 29.2 %collective-permute-start.15 = (bf16[2432,256]{1,0:T(8,128)(2,1)}, bf16[2432,256]{1,0:T(8,128)(2,1)}, u32[]{:S(2)}, u32[]{:S(2)}) collective-permute-start(bf16[2432,256]{1,0:T(8,128)(2,1)} %get-tuple-element.81), channel_id=1, source_target_pairs={{0,3},{1,0},{2,1},{3,2},{4,7},{5,4},{6,5},{7,6},{8,11},{9,8},{10,9... | collective-permute-start | bytes 3735560 | tf_op jit(solution)/shard_map/ppermute | solution.py:60
  85.9 28.9 %collective-permute-start.16 = (bf16[4,8,128,128]{3,2,1,0:T(8,128)(2,1)}, bf16[4,8,128,128]{3,2,1,0:T(8,128)(2,1)}, u32[]{:S(2)}, u32[]{:S(2)}) collective-permute-start(bf16[4,8,128,128]{3,2,1,0:T(8,128)(2,1)} %collective-permute-done.11.refs_2_), channel_id=1, source_target_pairs={{0,16},{16,0},{32,48},{48,32},{64,80},{80,64},{96,112},{112,96},{1... | collective-permute-start | bytes 3145736 | tf_op jit(solution)/shard_map/ppermute | solution.py:64
  85.9 20.5 %collective-permute-start.12 = (bf16[960,256]{1,0:T(8,128)(2,1)}, bf16[960,256]{1,0:T(8,128)(2,1)S(1)}, u32[]{:S(2)}, u32[]{:S(2)}) collective-permute-start(bf16[960,256]{1,0:T(8,128)(2,1)} %shard_map.105), channel_id=1, source_target_pairs={{0,4},{1,5},{2,6},{3,7},{4,8},{5,9},{6,10},{7,11},{8,12},{9,13},{1... | collective-permute-start | bytes 1474568 | tf_op jit(solution)/shard_map/ppermute | solution.py:60
  86.3 25.5 %collective-permute-start.13 = (bf16[960,256]{1,0:T(8,128)(2,1)}, bf16[960,256]{1,0:T(8,128)(2,1)}, u32[]{:S(2)}, u32[]{:S(2)}) collective-permute-start(bf16[960,256]{1,0:T(8,128)(2,1)} %shard_map.105), channel_id=1, source_target_pairs={{0,12},{1,13},{2,14},{3,15},{4,0},{5,1},{6,2},{7,3},{8,4},{9,5},{1... | collective-permute-start | bytes 1474568 | tf_op jit(solution)/shard_map/ppermute | solution.py:60
  114.8 9.0 %collective-permute-start.17 = (bf16[4,8,128,128]{3,2,1,0:T(8,128)(2,1)}, bf16[4,8,128,128]{3,2,1,0:T(8,128)(2,1)}, u32[]{:S(2)}, u32[]{:S(2)}) collective-permute-start(bf16[4,8,128,128]{3,2,1,0:T(8,128)(2,1)} %shard_map.103.refs_0_), channel_id=1, source_target_pairs={{0,16},{16,0},{32,48},{48,32},{64,80},{80,64},{96,112},{112,96},{1... | collective-permute-start | bytes 3145736 | tf_op jit(solution)/shard_map/ppermute | solution.py:64
  115.9 31.1 %collective-permute-start.18 = (bf16[1216,256]{1,0:T(8,128)(2,1)}, bf16[1216,256]{1,0:T(8,128)(2,1)S(1)}, u32[]{:S(2)}, u32[]{:S(2)}) collective-permute-start(bf16[1216,256]{1,0:T(8,128)(2,1)} %get-tuple-element.93), channel_id=1, source_target_pairs={{0,1},{1,2},{2,3},{3,0},{4,5},{5,6},{6,7},{7,4},{8,9},{9,10},{10,1... | collective-permute-start | bytes 1867784 | tf_op jit(solution)/shard_map/ppermute | solution.py:60
  116.0 31.0 %collective-permute-start.19 = (bf16[1216,256]{1,0:T(8,128)(2,1)}, bf16[1216,256]{1,0:T(8,128)(2,1)S(1)}, u32[]{:S(2)}, u32[]{:S(2)}) collective-permute-start(bf16[1216,256]{1,0:T(8,128)(2,1)} %get-tuple-element.94), channel_id=1, source_target_pairs={{0,3},{1,0},{2,1},{3,2},{4,7},{5,4},{6,5},{7,6},{8,11},{9,8},{10,9... | collective-permute-start | bytes 1867784 | tf_op jit(solution)/shard_map/ppermute | solution.py:60
  119.3 27.8 %collective-permute-start.20 = (bf16[640,256]{1,0:T(8,128)(2,1)}, bf16[640,256]{1,0:T(8,128)(2,1)S(1)}, u32[]{:S(2)}, u32[]{:S(2)}) collective-permute-start(bf16[640,256]{1,0:T(8,128)(2,1)} %get-tuple-element.95), channel_id=1, source_target_pairs={{0,4},{1,5},{2,6},{3,7},{4,8},{5,9},{6,10},{7,11},{8,12},{9,13},{1... | collective-permute-start | bytes 983048 | tf_op jit(solution)/shard_map/ppermute | solution.py:60
  123.0 24.1 %collective-permute-start.21 = (bf16[640,256]{1,0:T(8,128)(2,1)}, bf16[640,256]{1,0:T(8,128)(2,1)S(1)}, u32[]{:S(2)}, u32[]{:S(2)}) collective-permute-start(bf16[640,256]{1,0:T(8,128)(2,1)} %get-tuple-element.96), channel_id=1, source_target_pairs={{0,12},{1,13},{2,14},{3,15},{4,0},{5,1},{6,2},{7,3},{8,4},{9,5},{1... | collective-permute-start | bytes 983048 | tf_op jit(solution)/shard_map/ppermute | solution.py:60
  (25 other events, 321.7 us)
